TPU v7x, 32 devices: a whole 2x2x4 slice. The times are simulated.
32 devices in a mesh: tile: 16 (over z, x, core), tm: 2 (over y).
Axes of the slice: x: 2, y: 2, z: 4, core: 2. Of those that a mesh axis runs over, the one named last changes fastest.
Arguments:
- features: bfloat16 [192, 8, 16, 16, 128], P('tile', 'tm'), may hold values from -6 to 6
- weight_one: bfloat16 [3, 3, 128, 128], replicated, may hold values from -0.1875 to 0.1875
- bias_one: float32 [128], replicated, may hold values from -3 to 3
- weight_two: bfloat16 [3, 3, 128, 128], replicated, may hold values from -0.1875 to 0.1875
- bias_two: float32 [128], replicated, may hold values from -3 to 3
- cotangent: bfloat16 [192, 8, 16, 16, 128], P('tile', 'tm'), may hold values from -6 to 6
Outputs:
- output: bfloat16 [192, 8, 16, 16, 128], P('tile', 'tm')
- grad_weight_one: float32 [3, 3, 128, 128], replicated
- grad_bias_one: float32 [128], replicated
- grad_weight_two: float32 [3, 3, 128, 128], replicated
- grad_bias_two: float32 [128], replicated
All inputs are finite; a program needn't handle non-finite values.
Results may differ from a plain program's by a relative error of at most 0.0085.
Values may be sent and summed in bfloat16 or wider, within the bound.
A program may use at most 256 MiB of HBM per device.

v0:
```python
import math

import jax
import jax.numpy as jnp
import numpy as np
from jax import lax
from jax.sharding import PartitionSpec as P

S = 4


inv_sqrt_two = 0.7071067811865476
inv_sqrt_tau = 0.3989422804014327


def as_sent(x):

    def short(part):
        return part.astype(jnp.bfloat16) if part.dtype == jnp.float32 else part

    return jax.tree.map(short, x)


def passed_along(value, axis, steps):
    count = lax.axis_size(axis)
    pairs = [(source, (source + steps) % count) for source in range(count)]
    return lax.ppermute(value, axis, pairs)


def edge_partner(face_id, edge_id):
    group_id = face_id // 4
    within = face_id % 4
    after_id = (within + 1) % 4
    before = (within + 3) % 4
    if group_id == 0:
        options = [(after_id, 2), (4 + within, 0), (before, 0), (4 + after_id, 2)]
    elif group_id == 1:
        options = [(within, 1), (8 + before, 0), (before, 3), (8 + within, 2)]
    else:
        options = [(4 + after_id, 1), (8 + before, 3), (4 + within, 3), (8 + after_id, 1)]
    return options[edge_id]


def entry_pixel(edge_id, along_edge, length):
    if edge_id == 0:
        return (0, along_edge)
    if edge_id == 1:
        return (length - 1, along_edge)
    if edge_id == 2:
        return (along_edge, 0)
    return (along_edge, length - 1)


def step_pixel(face_id, row_at, col_at, row_step, col_step, length):
    row_new = row_at + row_step
    col_new = col_at + col_step
    if 0 <= row_new < length and 0 <= col_new < length:
        return (face_id, row_new, col_new, -1)
    if row_new < 0:
        edge_id = 0
    elif row_new >= length:
        edge_id = 1
    elif col_new < 0:
        edge_id = 2
    else:
        edge_id = 3
    along_edge = col_at if edge_id < 2 else row_at
    partner, entered = edge_partner(face_id, edge_id)
    row_in, col_in = entry_pixel(entered, along_edge, length)
    return (partner, row_in, col_in, entered)


def neighbour_pixel(face_id, row_at, col_at, row_step, col_step, length):
    if row_step == 0 or col_step == 0:
        found = step_pixel(face_id, row_at, col_at, row_step, col_step, length)
        return (found[0], found[1], found[2])
    face_one, row_one, col_one, entered = step_pixel(face_id, row_at, col_at, row_step, 0, length)
    if entered >= 2:
        found = step_pixel(face_one, row_one, col_one, col_step, 0, length)
    else:
        found = step_pixel(face_one, row_one, col_one, 0, col_step, length)
    return (found[0], found[1], found[2])


def tile_slot(face_id, tile_row, tile_col, side_tiles):
    group_id = face_id // 4
    within = face_id % 4
    extra = 1 if group_id == 2 else 0
    column = (side_tiles * (within + extra) + tile_col) % (4 * side_tiles)
    return 3 * side_tiles * column + side_tiles * group_id + tile_row


def cycle_position(row_at, col_at, pixels):
    if row_at == 0:
        return col_at
    if row_at == pixels - 1:
        return pixels + col_at
    if col_at == 0:
        return 2 * pixels + row_at - 1
    return 3 * pixels - 2 + row_at - 1


def halo_positions(pixels):
    places = [(-1, column) for column in range(-1, pixels + 1)]
    places = places + [(pixels, column) for column in range(-1, pixels + 1)]
    places = places + [(row_at, -1) for row_at in range(pixels)]
    places = places + [(row_at, pixels) for row_at in range(pixels)]
    return places


def halo_sources(side_tiles, pixels):
    slot_count = 12 * side_tiles * side_tiles
    places = halo_positions(pixels)
    length = side_tiles * pixels
    source_slot = np.zeros((slot_count, len(places)), np.int64)
    source_cycle = np.zeros((slot_count, len(places)), np.int64)
    for face_id in range(12):
        for tile_row in range(side_tiles):
            for tile_col in range(side_tiles):
                slot_id = tile_slot(face_id, tile_row, tile_col, side_tiles)
                for cell_index in range(len(places)):
                    row_at, col_at = places[cell_index]
                    inner_row = min(max(row_at, 0), pixels - 1)
                    inner_col = min(max(col_at, 0), pixels - 1)
                    partner, row_new, col_new = neighbour_pixel(
                        face_id,
                        tile_row * pixels + inner_row,
                        tile_col * pixels + inner_col,
                        row_at - inner_row,
                        col_at - inner_col,
                        length,
                    )
                    source_slot[slot_id, cell_index] = tile_slot(
                        partner, row_new // pixels, col_new // pixels, side_tiles
                    )
                    source_cycle[slot_id, cell_index] = cycle_position(
                        row_new % pixels, col_new % pixels, pixels
                    )
    return (source_slot, source_cycle)


def padded_rows(row_lists, filler):
    widest = max([len(one_row) for one_row in row_lists] + [1])
    return np.array(
        [list(one_row) + [filler] * (widest - len(one_row)) for one_row in row_lists], np.int32
    )


def device_tables(device_count, per_device, side_tiles, pixels):
    cycle_len = 4 * pixels - 4
    halo_len = 4 * pixels + 4
    source_slot, source_cycle = halo_sources(side_tiles, pixels)
    entries = []
    offset_set = set()
    for device in range(device_count):
        listing = []
        for local_id in range(per_device):
            slot_id = device * per_device + local_id
            for cell_index in range(halo_len):
                source = int(source_slot[slot_id, cell_index])
                owner_id = source // per_device
                moved_by = (device - owner_id) % device_count
                if moved_by > device_count // 2:
                    moved_by = moved_by - device_count
                cycle_index = source % per_device * cycle_len + int(
                    source_cycle[slot_id, cell_index]
                )
                listing.append((local_id * halo_len + cell_index, moved_by, cycle_index))
                if moved_by != 0:
                    offset_set.add(moved_by)
        entries.append(listing)
    offsets = [int(value_at) for value_at in sorted(offset_set)]
    cycle_dummy = per_device * cycle_len
    halo_dummy = per_device * halo_len
    receive = np.zeros((device_count, halo_dummy), np.int32)
    for device in range(device_count):
        for record in entries[device]:
            if record[1] == 0:
                receive[device, record[0]] = record[2]
    local_halo = padded_rows(
        [[record[0] for record in listing if record[1] == 0] for listing in entries], halo_dummy
    )
    local_cycle = padded_rows(
        [[record[2] for record in listing if record[1] == 0] for listing in entries], cycle_dummy
    )
    forward_rows = []
    back_rows = []
    target_rows = []
    base_at = cycle_dummy + 1
    for offset in offsets:
        chosen = [
            [(record[0], record[2]) for record in listing if record[1] == offset]
            for listing in entries
        ]
        widest = max([len(pick_list) for pick_list in chosen] + [1])
        send_table = np.full((device_count, widest), cycle_dummy, np.int32)
        back_table = np.full((device_count, widest), halo_dummy, np.int32)
        for device in range(device_count):
            sender = (device - offset) % device_count
            for position in range(len(chosen[device])):
                halo_index, cycle_index = chosen[device][position]
                send_table[sender, position] = cycle_index
                back_table[device, position] = halo_index
                receive[device, halo_index] = base_at + position
        forward_rows.append(send_table)
        back_rows.append(back_table)
        target_rows.append(send_table)
        base_at = base_at + widest
    return (offsets, forward_rows, receive, back_rows, target_rows, local_halo, local_cycle)


def select_row(table_np, tile_index):
    return jnp.asarray(table_np, dtype=jnp.int32)[tile_index]


def rim_of(tile_data):
    pixels = tile_data.shape[2]
    pieces = [
        tile_data[:, :, 0],
        tile_data[:, :, pixels - 1],
        tile_data[:, :, 1 : pixels - 1, 0],
        tile_data[:, :, 1 : pixels - 1, pixels - 1],
    ]
    joined = jnp.concatenate(pieces, axis=2).transpose(0, 2, 1, 3)
    return joined.reshape((-1,) + joined.shape[2:])


def border_of(padded):
    edge_at = padded.shape[2] - 1
    pieces = [
        padded[:, :, 0],
        padded[:, :, edge_at],
        padded[:, :, 1:edge_at, 0],
        padded[:, :, 1:edge_at, edge_at],
    ]
    joined = jnp.concatenate(pieces, axis=2).transpose(0, 2, 1, 3)
    return joined.reshape((-1,) + joined.shape[2:])


def attach_border(tile_data, border, pixels):
    per_device = tile_data.shape[0]
    halo_cells = border.reshape((per_device, 4 * pixels + 4) + border.shape[1:]).transpose(
        0, 2, 1, 3
    )
    top_row = halo_cells[:, :, 0 : pixels + 2]
    bottom_row = halo_cells[:, :, pixels + 2 : 2 * pixels + 4]
    left_col = halo_cells[:, :, 2 * pixels + 4 : 3 * pixels + 4]
    right_col = halo_cells[:, :, 3 * pixels + 4 :]
    middle = jnp.concatenate([left_col[:, :, :, None], tile_data, right_col[:, :, :, None]], axis=3)
    return jnp.concatenate([top_row[:, :, None], middle, bottom_row[:, :, None]], axis=2)


def add_rim(inner_part, rim_grad, pixels):
    per_device = inner_part.shape[0]
    rim_cells = rim_grad.reshape((per_device, 4 * pixels - 4) + rim_grad.shape[1:]).transpose(
        0, 2, 1, 3
    )
    inner_part = inner_part.at[:, :, 0].add(rim_cells[:, :, 0:pixels])
    inner_part = inner_part.at[:, :, pixels - 1].add(rim_cells[:, :, pixels : 2 * pixels])
    inner_part = inner_part.at[:, :, 1 : pixels - 1, 0].add(
        rim_cells[:, :, 2 * pixels : 3 * pixels - 2]
    )
    inner_part = inner_part.at[:, :, 1 : pixels - 1, pixels - 1].add(
        rim_cells[:, :, 3 * pixels - 2 :]
    )
    return inner_part


def gelu_exact(value):
    return 0.5 * value * (1.0 + lax.erf(value * inv_sqrt_two))


def gelu_slope(value):
    return (
        0.5 * (1.0 + lax.erf(value * inv_sqrt_two))
        + value * jnp.exp(-0.5 * value * value) * inv_sqrt_tau
    )


def conv_columns(padded, pixels):
    pieces = []
    for row_off in range(3):
        for col_off in range(3):
            pieces.append(padded[..., row_off : row_off + pixels, col_off : col_off + pixels, :])
    joined = jnp.concatenate(pieces, axis=-1)
    return joined.reshape(-1, joined.shape[-1])


def spread_back(columns, lead, pixels, channels):
    parts = columns.reshape(lead + (pixels, pixels, 9, channels))
    total_sum = jnp.zeros(lead + (pixels + 2, pixels + 2, channels), jnp.float32)
    for row_off in range(3):
        for col_off in range(3):
            widths = [(0, 0)] * len(lead) + [(row_off, 2 - row_off), (col_off, 2 - col_off), (0, 0)]
            total_sum = total_sum + jnp.pad(parts[..., row_off * 3 + col_off, :], widths)
    return total_sum


def fill_border(tile_data, layout, tile_index):
    offsets = layout[0]
    forward_rows = layout[1]
    pixels = tile_data.shape[2]
    rim_data = rim_of(tile_data)
    rim_ext = jnp.concatenate(
        [rim_data, jnp.zeros((1,) + rim_data.shape[1:], rim_data.dtype)], axis=0
    )
    pieces = [rim_ext]
    for position in range(len(offsets)):
        if forward_rows[position] is None:
            outgoing = rim_data
        else:
            outgoing = jnp.take(rim_ext, select_row(forward_rows[position], tile_index), axis=0)
        pieces.append(
            passed_along(as_sent(outgoing), "tile", offsets[position]).astype(outgoing.dtype)
        )
    pool_data = jnp.concatenate(pieces, axis=0)
    border = jnp.take(pool_data, select_row(layout[2], tile_index), axis=0)
    return attach_border(tile_data, border, pixels)


def fold_border(grad_pad, layout, tile_index):
    offsets = layout[0]
    back_rows = layout[3]
    target_rows = layout[4]
    pixels = grad_pad.shape[2] - 2
    per_device = grad_pad.shape[0]
    inner_part = grad_pad[:, :, 1:-1, 1:-1]
    border = lax.optimization_barrier(border_of(grad_pad).astype(jnp.bfloat16))
    border_ext = jnp.concatenate([border, jnp.zeros((1,) + border.shape[1:], border.dtype)], axis=0)
    rim_grad = jnp.zeros((per_device * (4 * pixels - 4) + 1,) + border.shape[1:], jnp.float32)
    local_terms = jnp.take(border_ext, select_row(layout[5], tile_index), axis=0)
    rim_grad = rim_grad.at[select_row(layout[6], tile_index)].add(local_terms.astype(jnp.float32))
    for position in range(len(offsets)):
        if back_rows[position] is None:
            outgoing = border
        else:
            outgoing = jnp.take(border_ext, select_row(back_rows[position], tile_index), axis=0)
        incoming = passed_along(outgoing, "tile", -offsets[position])
        rim_grad = rim_grad.at[select_row(target_rows[position], tile_index)].add(
            incoming.astype(jnp.float32)
        )
    return add_rim(inner_part, rim_grad[:-1], pixels)


def process(
    features_part, cotangent_part, weight_one, bias_one, weight_two, bias_two, layout, tile_index
):
    full_shape = features_part.shape
    pixels = full_shape[2]
    channels = full_shape[4]
    lead = full_shape[:2]
    mat_one = weight_one.reshape(9 * channels, channels)
    mat_two = weight_two.reshape(9 * channels, channels)
    columns_one = conv_columns(fill_border(features_part, layout, tile_index), pixels)
    pre_one = jnp.dot(columns_one, mat_one, preferred_element_type=jnp.float32) + bias_one
    hidden = gelu_exact(pre_one).astype(jnp.bfloat16).reshape(full_shape)
    columns_two = conv_columns(fill_border(hidden, layout, tile_index), pixels)
    pre_two = jnp.dot(columns_two, mat_two, preferred_element_type=jnp.float32) + bias_two
    output = gelu_exact(pre_two).astype(jnp.bfloat16)
    delta_two = (
        cotangent_part.reshape(-1, channels).astype(jnp.float32) * gelu_slope(pre_two)
    ).astype(jnp.bfloat16)
    grad_w_two = lax.dot_general(
        columns_two, delta_two, (((0,), (0,)), ((), ())), preferred_element_type=jnp.float32
    )
    grad_b_two = jnp.sum(delta_two.astype(jnp.float32), axis=0)
    back_two = lax.dot_general(
        delta_two, mat_two, (((1,), (1,)), ((), ())), preferred_element_type=jnp.float32
    )
    grad_hidden = fold_border(spread_back(back_two, lead, pixels, channels), layout, tile_index)
    delta_one = (grad_hidden.reshape(-1, channels) * gelu_slope(pre_one)).astype(jnp.bfloat16)
    grad_w_one = lax.dot_general(
        columns_one, delta_one, (((0,), (0,)), ((), ())), preferred_element_type=jnp.float32
    )
    grad_b_one = jnp.sum(delta_one.astype(jnp.float32), axis=0)
    return (output.reshape(full_shape), (grad_w_one, grad_b_one, grad_w_two, grad_b_two))


def body(features, weight_one, bias_one, weight_two, bias_two, cotangent):
    device_count = lax.axis_size("tile")
    tile_index = lax.axis_index("tile")
    per_device = features.shape[0]
    batch_size = features.shape[1]
    pixels = features.shape[2]
    channels = features.shape[4]
    layout = device_tables(device_count, per_device, S, pixels)
    output, grad_terms = process(
        features, cotangent, weight_one, bias_one, weight_two, bias_two, layout, tile_index
    )
    total_pixels = 12 * S * S * pixels * pixels * batch_size * lax.axis_size("tm")
    grad_scale = 1.0 / math.sqrt(total_pixels)
    totals = lax.psum((grad_terms[0], grad_terms[1], grad_terms[2], grad_terms[3]), ("tile", "tm"))
    grad_weight_one = (totals[0] * grad_scale).reshape(3, 3, channels, channels)
    grad_bias_one = totals[1] * grad_scale
    grad_weight_two = (totals[2] * grad_scale).reshape(3, 3, channels, channels)
    grad_bias_two = totals[3] * grad_scale
    return (output, grad_weight_one, grad_bias_one, grad_weight_two, grad_bias_two)


def solution(mesh):
    return jax.shard_map(
        body,
        mesh=mesh,
        in_specs=(
            P("tile", "tm", None, None, None),
            P(),
            P(),
            P(),
            P(),
            P("tile", "tm", None, None, None),
        ),
        out_specs=(P("tile", "tm", None, None, None), P(), P(), P(), P()),
        check_vma=False,
    )
```

profile of v0, /device:TPU:0, one launch (start us, length us, event | category | flops | bytes accessed | tf_op | source)
XLA Modules:
  0.0 647.0 jit_solution(16530726184985342912)
XLA Ops:
  15.5 4.0 collective-permute-start.8
  64.6 2.7 gather_fusion.5
  67.3 2.7 gather_fusion.4
  80.2 4.4 collective-permute-start.3
  89.0 4.2 collective-permute-done.4
  97.8 4.3 gather_fusion.9
  102.1 4.3 broadcast_select_fusion
  107.6 6.5 %pad_maximum_fusion = (bf16[12,4,17,18,128]{4,3,2,1,0:T(8,128)(2,1)S(1)}, bf16[12,4,17,18,128]{4,3,2,1,0:T(8,128)(2,1)S(1)}) fusion(bf16[12,4,1,18,128]{4,3,2,1,0:T(8,128)(2,1)S(1)} %copy.87, bf16[12,4,16,1,128]{4,3,2,1,0:T(2,128)(2,1)S(1)} %copy.83, bf16[12,4,16,16,128]{4,3,2,1,0:T(8,128)(2,1)S(1)} %copy-done.2, bf16[12,4,16,1,128]{4,3,2,1,0:T(2,128)(2,1)S(1)} %copy.82, ...), kind=kLoop, calls=%fused_computation.69 | loop fusion | flops 30081024 | bytes 11501568 | tf_op jit(solution)/shard_map/concatenate | solution.py:250
  114.1 2.7 slice_dynamic-update-slice_fusion.5
  116.8 3.4 slice_dynamic-update-slice_fusion.4
  120.2 3.3 slice_dynamic-update-slice_fusion.3
  123.5 3.1 fusion.13
  129.0 3.7 fusion.12
  132.7 2.6 slice_dynamic-update-slice_fusion.2
  135.3 3.3 slice_dynamic-update-slice_fusion.1
  138.7 3.4 slice_dynamic-update-slice_fusion
  142.0 14.9 %multiply_convert_fusion.1 = (bf16[12288,128]{1,0:T(8,128)(2,1)S(1)}, f32[12288,128]{1,0:T(8,128)}) fusion(f32[128]{0:T(128)S(1)} %copy-done.39, bf16[12288,1152]{1,0:T(8,128)(2,1)} %bitcast.298, bf16[1152,128]{1,0:T(8,128)(2,1)S(1)} %bitcast.310), kind=kOutput, calls=%fused_computation.66 | convolution fusion | flops 3633315840 | bytes 38044160 | tf_op jit(solution)/shard_map/dot_general | solution.py:355
  172.0 2.7 gather_fusion.14
  174.7 2.7 gather_fusion.13
  193.6 4.3 collective-permute-start.12
  202.3 4.5 collective-permute-done.13
  209.9 4.3 gather_fusion.18
  214.2 4.5 broadcast_select_fusion.1
  219.9 5.0 pad_maximum_fusion.2
  224.8 6.0 pad_maximum_fusion.1
  252.5 17.0 %convert_reduce_fusion = (f32[128]{0:T(128)S(1)}, bf16[12288,128]{1,0:T(8,128)(2,1)S(1)}, bf16[12288,128]{1,0:T(8,128)(2,1)}) fusion(bf16[12,4,16,16,128]{4,3,2,1,0:T(8,128)(2,1)S(1)} %copy-done.37, f32[128]{0:T(128)S(1)} %copy-done.40, bf16[12288,1152]{1,0:T(8,128)(2,1)} %constant_dynamic-update-slice_fusion.23, bf16[1152,128]{1,0:T(8,128)(2,1)S(1)} %bitcast.255), kind=kOutput, calls=%fused_computation.62 | convolution fusion | flops 3650617344 | bytes 38044672 | tf_op jit(solution)/shard_map/dot_general | solution.py:358
  269.6 13.5 %fusion.48 = f32[1152,128]{1,0:T(8,128)} fusion(bf16[12288,1152]{1,0:T(8,128)(2,1)} %constant_dynamic-update-slice_fusion.23, bf16[12288,128]{1,0:T(8,128)(2,1)S(1)} %get-tuple-element.100), kind=kOutput, calls=%fused_computation.299 | convolution fusion | flops 3623878656 | bytes 32047104 | tf_op jit(solution)/shard_map/dot_general | solution.py:363
  283.0 20.2 %fusion.46 = f32[12,4,16,16,9,128]{5,3,4,2,1,0:T(8,128)} fusion(bf16[12,4,16,16,128,1]{4,3,5,2,1,0:T(8,128)(2,1)S(1)} %bitcast.284, bf16[9,128,128,1,1,1]{2,1,0,5,4,3:T(8,128)(2,1)S(1)} %bitcast.256), kind=kOutput, calls=%fused_computation.297 | convolution fusion | flops 3623878656 | bytes 60063744 | tf_op jit(solution)/shard_map/dot_general | solution.py:367
  303.3 37.5 %slice_bitcast_fusion.8 = (f32[12,4,16,16,128]{4,3,2,1,0:T(8,128)}, f32[12,4,16,16,128]{4,3,2,1,0:T(8,128)}, f32[12,4,16,16,128]{4,3,2,1,0:T(8,128)}, f32[12,4,1...) fusion(f32[12,4,16,16,9,128]{5,3,4,2,1,0:T(8,128)} %fusion.46), kind=kLoop, calls=%fused_computation.61 | loop fusion | bytes 113246208 | tf_op jit(solution)/shard_map/squeeze | solution.py:295
  340.8 23.6 %fusion.39 = (bf16[12,4,18,18,128]{4,3,2,1,0:T(8,128)(2,1)S(1)}, f32[12,4,18,18,128]{4,3,2,1,0:T(8,128)}) fusion(f32[12,4,16,16,128]{4,3,2,1,0:T(8,128)} %get-tuple-element.136, f32[12,4,16,16,128]{4,3,2,1,0:T(8,128)} %get-tuple-element.137, f32[12,4,16,16,128]{4,3,2,1,0:T(8,128)} %get-tuple-element.130, f32[12,4,16,16,128]{4,3,2,1,0:T(8,128)} %get-tuple-element.131, ...), kind=kLoop, calls=%fused_computation.290 | loop fusion | flops 17915904 | bytes 68567040 | tf_op jit(solution)/shard_map/convert.12
  372.1 3.8 collective-permute-start.25
  381.6 4.5 collective-permute-start.22
  388.8 4.7 collective-permute-start.23
  393.5 4.6 slice.493
  398.2 4.6 copy.130
  403.0 13.1 %scatter_fusion = f32[721,4,128]{2,1,0:T(4,128)S(1)} fusion(f32[721,4,128]{2,1,0:T(4,128)S(1)} %broadcast_in_dim.141, s32[352]{0:T(512)S(1)} %copy-done.9, f32[352,4,128]{2,1,0:T(4,128)S(1)} %select_convert_fusion), kind=kCustom, calls=%fused_computation.27 | custom fusion | flops 180224 | bytes 2164096 | tf_op jit(solution)/shard_map/scatter-add | solution.py:332
  422.8 8.4 %scatter_fusion.4 = f32[721,4,128]{2,1,0:T(4,128)S(1)} fusion(f32[721,4,128]{2,1,0:T(4,128)S(1)} %scatter_fusion.3, s32[214]{0:T(256)S(1)} %bitcast.309, f32[214,4,128]{2,1,0:T(4,128)S(1)} %convert_element_type.90), kind=kCustom, calls=%fused_computation.31 | custom fusion | flops 109568 | bytes 1315672 | tf_op jit(solution)/shard_map/scatter-add | solution.py:339
  431.3 8.3 %scatter_fusion.5 = f32[721,4,128]{2,1,0:T(4,128)S(1)} fusion(f32[721,4,128]{2,1,0:T(4,128)S(1)} %scatter_fusion.4, s32[214]{0:T(256)S(1)} %bitcast.308, f32[214,4,128]{2,1,0:T(4,128)S(1)} %convert_element_type.91), kind=kCustom, calls=%fused_computation.32 | custom fusion | flops 109568 | bytes 1315672 | tf_op jit(solution)/shard_map/scatter-add | solution.py:339
  448.7 9.6 %scatter-add.98 = f32[12,4,16,16,128]{4,2,1,0,3:T(8,128)} dynamic-update-slice(f32[12,4,16,16,128]{4,2,1,0,3:T(8,128)} %copy.130, f32[12,4,1,16,128]{4,2,1,0,3:T(1,128)S(1)} %copy.110, s32[]{:T(128)} %constant.311.clone.1, s32[]{:T(128)} %constant.311.clone.1, s32[]{:T(128)} %constant.311.clone.1, s32[]{:T(128)} %constant.311.clone.1, s32[]{:T(128)} %constant.311.clone.1) | dynamic-update-slice | bytes 786436 | tf_op jit(solution)/shard_map/scatter-add | solution.py:258
  458.3 2.5 slice_add_fusion
  460.8 9.6 %scatter-add.99 = f32[12,4,16,16,128]{4,2,1,0,3:T(8,128)} dynamic-update-slice(f32[12,4,16,16,128]{4,2,1,0,3:T(8,128)} %scatter-add.98, f32[12,4,1,16,128]{4,2,1,0,3:T(1,128)S(1)} %slice_add_fusion, s32[]{:T(128)} %constant.311.clone.1, s32[]{:T(128)} %constant.311.clone.1, s32[]{:T(128)} %constant.330.clone.1, s32[]{:T(128)} %constant.311.clone.1, s32[]{:T(128)} %constant.311.clone.1) | dynamic-update-slice | bytes 786436 | tf_op jit(solution)/shard_map/scatter-add | solution.py:259
  471.6 3.2 scatter-add.100
  476.0 3.5 scatter-add.101
  479.5 7.3 %copy.112 = f32[12,4,16,16,128]{4,3,2,1,0:T(8,128)S(1)} copy(f32[12,4,16,16,128]{4,2,1,0,3:T(8,128)} %scatter-add.101) | data formatting | bytes 12582912 | tf_op jit(solution)/shard_map/scatter-add | solution.py:263
  486.9 3.0 convert_reduce_fusion.1
  489.9 13.6 %fusion.47 = f32[1152,128]{1,0:T(8,128)} fusion(bf16[12288,1152]{1,0:T(8,128)(2,1)} %bitcast.299, bf16[12288,128]{1,0:T(8,128)(2,1)S(1)} %get-tuple-element.102), kind=kOutput, calls=%fused_computation.298 | convolution fusion | flops 3623878656 | bytes 32047104 | tf_op jit(solution)/shard_map/dot_general | solution.py:372
  503.5 40.2 %all-reduce.12 = (f32[128]{0:T(128)S(1)}, f32[128]{0:T(128)S(1)}) all-reduce(f32[128]{0:T(128)S(1)} %get-tuple-element.101, f32[128]{0:T(128)S(1)} %get-tuple-element.99), channel_id=1, replica_groups=mesh['tile'=16,'tm'=2] {'tile','tm'}, use_global_device_ids=true, to_apply=%region_12.21 | all-reduce | flops 256 | bytes 2048 | tf_op jit(solution)/shard_map/psum | solution.py:392
  544.7 91.1 %all-reduce.16.cloned.1.call-done = (f32[1152,128]{1,0:T(8,128)}, f32[1152,128]{1,0:T(8,128)}) async-done(((f32[1152,128]{1,0:T(8,128)}, f32[1152,128]{1,0:T(8,128)}), (f32[1152,128]{1,0:T(8,128)}, f32[1152,128]{1,0:T(8,128)})) %all-reduce.16.cloned.1.call-update) | async-done | bytes 1179664 | tf_op jit(solution)/shard_map/psum | solution.py:392
  (330 shorter events, 172.5 us)
Async XLA Ops:
  7.2 245.4 %copy-start = (bf16[3,3,128,128]{3,2,1,0:T(8,128)(2,1)S(1)}, bf16[3,3,128,128]{3,2,1,0:T(8,128)(2,1)}, u32[]{:S(2)}) copy-start(bf16[3,3,128,128]{3,2,1,0:T(8,128)(2,1)} %param.75) | copy-start | bytes 884740
  7.2 628.7 %all-reduce.16.cloned.1.call-start = ((), (), s32[]{:S(2)}) async-start(), calls=%async_computation | async-start | bytes 2359296 | tf_op jit(solution)/shard_map/psum | solution.py:392
  8.3 41.7 %copy-start.36 = (s32[3]{0:T(128)S(1)}, s32[3]{0:T(128)}, u32[]{:S(2)}) copy-start(s32[3]{0:T(128)} %constant.325.clone.1) | copy-start | bytes 40
  15.5 81.1 %collective-permute-start.8 = (bf16[1,4,128]{2,1,0:T(4,128)(2,1)}, bf16[1,4,128]{2,1,0:T(4,128)(2,1)}, u32[]{:S(2)}, u32[]{:S(2)}) collective-permute-start(bf16[1,4,128]{2,1,0:T(4,128)(2,1)} %fusion.24), channel_id=1, source_target_pairs={{0,16},{2,18},{4,20},{6,22},{8,24},{10,26},{12,28},{14,30},{16,0},... | collective-permute-start | bytes 3080 | tf_op jit(solution)/shard_map/ppermute | solution.py:27
  20.3 28.6 %copy-start.10 = (s32[1024]{0:T(1024)}, s32[1024]{0:T(1024)S(1)}, u32[]{:S(2)}) copy-start(s32[1024]{0:T(1024)S(1)} %pad_clamp_fusion.17) | copy-start | bytes 12292
  20.6 28.3 %copy-start.7 = (bf16[721,4,128]{2,1,0:T(4,128)(2,1)}, bf16[721,4,128]{2,1,0:T(4,128)(2,1)S(1)}, u32[]{:S(2)}) copy-start(bf16[721,4,128]{2,1,0:T(4,128)(2,1)S(1)} %concatenate.105) | copy-start | bytes 2214916
  21.9 57.0 %collective-permute-start = (bf16[17,4,128]{2,1,0:T(4,128)(2,1)}, bf16[17,4,128]{2,1,0:T(4,128)(2,1)}, u32[]{:S(2)}, u32[]{:S(2)}) collective-permute-start(bf16[17,4,128]{2,1,0:T(4,128)(2,1)} %broadcast_select_fusion.25), channel_id=1, source_target_pairs={{0,24},{2,26},{4,28},{6,30},{8,0},{10,2},{12,4},{14,6},{16,8},{18,... | collective-permute-start | bytes 52232 | tf_op jit(solution)/shard_map/ppermute | solution.py:27
  23.2 25.6 %copy-start.11 = (s32[1024]{0:T(1024)}, s32[1024]{0:T(1024)S(1)}, u32[]{:S(2)}) copy-start(s32[1024]{0:T(1024)S(1)} %pad_clamp_fusion.10) | copy-start | bytes 12292
  24.5 70.7 %collective-permute-start.7 = (bf16[17,4,128]{2,1,0:T(4,128)(2,1)}, bf16[17,4,128]{2,1,0:T(4,128)(2,1)}, u32[]{:S(2)}, u32[]{:S(2)}) collective-permute-start(bf16[17,4,128]{2,1,0:T(4,128)(2,1)} %broadcast_select_fusion.23), channel_id=1, source_target_pairs={{0,8},{2,10},{4,12},{6,14},{8,16},{10,18},{12,20},{14,22},{16,24},... | collective-permute-start | bytes 52232 | tf_op jit(solution)/shard_map/ppermute | solution.py:27
  25.9 22.9 %copy-start.18 = (pred[18]{0:T(512)(128)(4,1)}, pred[18]{0:T(512)(128)(4,1)S(1)}, u32[]{:S(2)}) copy-start(pred[18]{0:T(512)(128)(4,1)S(1)} %get-tuple-element.123) | copy-start | bytes 58
  26.0 22.9 %copy-start.12 = (s32[1024]{0:T(1024)}, s32[1024]{0:T(1024)S(1)}, u32[]{:S(2)}) copy-start(s32[1024]{0:T(1024)S(1)} %pad_clamp_fusion.16) | copy-start | bytes 12292
  27.3 52.9 %collective-permute-start.1 = (bf16[18,4,128]{2,1,0:T(4,128)(2,1)}, bf16[18,4,128]{2,1,0:T(4,128)(2,1)S(1)}, u32[]{:S(2)}, u32[]{:S(2)}) collective-permute-start(bf16[18,4,128]{2,1,0:T(4,128)(2,1)} %broadcast_select_fusion.19), channel_id=1, source_target_pairs={{0,26},{2,28},{4,30},{6,0},{8,2},{10,4},{12,6},{14,8},{16,10},{18,... | collective-permute-start | bytes 55304 | tf_op jit(solution)/shard_map/ppermute | solution.py:27
  29.7 55.5 %collective-permute-start.2 = (bf16[18,4,128]{2,1,0:T(4,128)(2,1)S(1)}, bf16[18,4,128]{2,1,0:T(4,128)(2,1)S(1)}, u32[]{:S(2)}, u32[]{:S(2)}) collective-permute-start(bf16[18,4,128]{2,1,0:T(4,128)(2,1)S(1)} %broadcast_select_fusion.17), channel_id=1, source_target_pairs={{0,28},{2,30},{4,0},{6,2},{8,4},{10,6},{12,8},{14,10},{16,12},{18,... | collective-permute-start | bytes 55304 | tf_op jit(solution)/shard_map/ppermute | solution.py:27
  50.0 57.6 %copy-start.2 = (bf16[12,4,16,16,128]{4,3,2,1,0:T(8,128)(2,1)S(1)}, bf16[12,4,16,16,128]{4,3,2,1,0:T(8,128)(2,1)}, u32[]{:S(2)}) copy-start(bf16[12,4,16,16,128]{4,3,2,1,0:T(8,128)(2,1)} %param.72) | copy-start | bytes 9437188
  78.9 15.2 %collective-permute-start.5 = (bf16[18,4,128]{2,1,0:T(4,128)(2,1)S(1)}, bf16[18,4,128]{2,1,0:T(4,128)(2,1)S(1)}, u32[]{:S(2)}, u32[]{:S(2)}) collective-permute-start(bf16[18,4,128]{2,1,0:T(4,128)(2,1)S(1)} %broadcast_select_fusion.15), channel_id=1, source_target_pairs={{0,4},{2,6},{4,8},{6,10},{8,12},{10,14},{12,16},{14,18},{16,20},{1... | collective-permute-start | bytes 55304 | tf_op jit(solution)/shard_map/ppermute | solution.py:27
  80.2 8.1 %collective-permute-start.3 = (bf16[214,4,128]{2,1,0:T(4,128)(2,1)S(1)}, bf16[214,4,128]{2,1,0:T(4,128)(2,1)S(1)}, u32[]{:S(2)}, u32[]{:S(2)}) collective-permute-start(bf16[214,4,128]{2,1,0:T(4,128)(2,1)S(1)} %broadcast_select_fusion.7), channel_id=1, source_target_pairs={{0,30},{2,0},{4,2},{6,4},{8,6},{10,8},{12,10},{14,12},{16,14},{18,... | collective-permute-start | bytes 657416 | tf_op jit(solution)/shard_map/ppermute | solution.py:27
  85.2 8.1 %collective-permute-start.4 = (bf16[214,4,128]{2,1,0:T(4,128)(2,1)S(1)}, bf16[214,4,128]{2,1,0:T(4,128)(2,1)S(1)}, u32[]{:S(2)}, u32[]{:S(2)}) collective-permute-start(bf16[214,4,128]{2,1,0:T(4,128)(2,1)S(1)} %broadcast_select_fusion.5), channel_id=1, source_target_pairs={{0,2},{2,4},{4,6},{6,8},{8,10},{10,12},{12,14},{14,16},{16,18},{18... | collective-permute-start | bytes 657416 | tf_op jit(solution)/shard_map/ppermute | solution.py:27
  88.3 6.4 collective-permute-start.6
  179.7 29.6 %collective-permute-start.17 = (bf16[1,4,128]{2,1,0:T(4,128)(2,1)}, bf16[1,4,128]{2,1,0:T(4,128)(2,1)S(1)}, u32[]{:S(2)}, u32[]{:S(2)}) collective-permute-start(bf16[1,4,128]{2,1,0:T(4,128)(2,1)} %fusion.23), channel_id=1, source_target_pairs={{0,16},{2,18},{4,20},{6,22},{8,24},{10,26},{12,28},{14,30},{16,0},... | collective-permute-start | bytes 3080 | tf_op jit(solution)/shard_map/ppermute | solution.py:27
  184.1 7.4 %collective-permute-start.9 = (bf16[17,4,128]{2,1,0:T(4,128)(2,1)S(1)}, bf16[17,4,128]{2,1,0:T(4,128)(2,1)S(1)}, u32[]{:S(2)}, u32[]{:S(2)}) collective-permute-start(bf16[17,4,128]{2,1,0:T(4,128)(2,1)S(1)} %broadcast_select_fusion.24), channel_id=1, source_target_pairs={{0,24},{2,26},{4,28},{6,30},{8,0},{10,2},{12,4},{14,6},{16,8},{18,... | collective-permute-start | bytes 52232 | tf_op jit(solution)/shard_map/ppermute | solution.py:27
  185.0 23.7 %collective-permute-start.16 = (bf16[17,4,128]{2,1,0:T(4,128)(2,1)S(1)}, bf16[17,4,128]{2,1,0:T(4,128)(2,1)S(1)}, u32[]{:S(2)}, u32[]{:S(2)}) collective-permute-start(bf16[17,4,128]{2,1,0:T(4,128)(2,1)S(1)} %broadcast_select_fusion.22), channel_id=1, source_target_pairs={{0,8},{2,10},{4,12},{6,14},{8,16},{10,18},{12,20},{14,22},{16,24},... | collective-permute-start | bytes 52232 | tf_op jit(solution)/shard_map/ppermute | solution.py:27
  186.1 7.5 %collective-permute-start.10 = (bf16[18,4,128]{2,1,0:T(4,128)(2,1)S(1)}, bf16[18,4,128]{2,1,0:T(4,128)(2,1)S(1)}, u32[]{:S(2)}, u32[]{:S(2)}) collective-permute-start(bf16[18,4,128]{2,1,0:T(4,128)(2,1)S(1)} %broadcast_select_fusion.18), channel_id=1, source_target_pairs={{0,26},{2,28},{4,30},{6,0},{8,2},{10,4},{12,6},{14,8},{16,10},{18,... | collective-permute-start | bytes 55304 | tf_op jit(solution)/shard_map/ppermute | solution.py:27
  187.9 10.6 %collective-permute-start.11 = (bf16[18,4,128]{2,1,0:T(4,128)(2,1)S(1)}, bf16[18,4,128]{2,1,0:T(4,128)(2,1)S(1)}, u32[]{:S(2)}, u32[]{:S(2)}) collective-permute-start(bf16[18,4,128]{2,1,0:T(4,128)(2,1)S(1)} %broadcast_select_fusion.16), channel_id=1, source_target_pairs={{0,28},{2,30},{4,0},{6,2},{8,4},{10,6},{12,8},{14,10},{16,12},{18,... | collective-permute-start | bytes 55304 | tf_op jit(solution)/shard_map/ppermute | solution.py:27
  191.5 16.0 %collective-permute-start.14 = (bf16[18,4,128]{2,1,0:T(4,128)(2,1)S(1)}, bf16[18,4,128]{2,1,0:T(4,128)(2,1)S(1)}, u32[]{:S(2)}, u32[]{:S(2)}) collective-permute-start(bf16[18,4,128]{2,1,0:T(4,128)(2,1)S(1)} %broadcast_select_fusion.14), channel_id=1, source_target_pairs={{0,4},{2,6},{4,8},{6,10},{8,12},{10,14},{12,16},{14,18},{16,20},{1... | collective-permute-start | bytes 55304 | tf_op jit(solution)/shard_map/ppermute | solution.py:27
  193.6 7.9 %collective-permute-start.12 = (bf16[214,4,128]{2,1,0:T(4,128)(2,1)S(1)}, bf16[214,4,128]{2,1,0:T(4,128)(2,1)S(1)}, u32[]{:S(2)}, u32[]{:S(2)}) collective-permute-start(bf16[214,4,128]{2,1,0:T(4,128)(2,1)S(1)} %broadcast_select_fusion.6), channel_id=1, source_target_pairs={{0,30},{2,0},{4,2},{6,4},{8,6},{10,8},{12,10},{14,12},{16,14},{18,... | collective-permute-start | bytes 657416 | tf_op jit(solution)/shard_map/ppermute | solution.py:27
  198.5 8.2 %collective-permute-start.13 = (bf16[214,4,128]{2,1,0:T(4,128)(2,1)S(1)}, bf16[214,4,128]{2,1,0:T(4,128)(2,1)S(1)}, u32[]{:S(2)}, u32[]{:S(2)}) collective-permute-start(bf16[214,4,128]{2,1,0:T(4,128)(2,1)S(1)} %broadcast_select_fusion.4), channel_id=1, source_target_pairs={{0,2},{2,4},{4,6},{6,8},{8,10},{10,12},{12,14},{14,16},{16,18},{18... | collective-permute-start | bytes 657416 | tf_op jit(solution)/shard_map/ppermute | solution.py:27
  201.5 6.6 %collective-permute-start.15 = (bf16[18,4,128]{2,1,0:T(4,128)(2,1)S(1)}, bf16[18,4,128]{2,1,0:T(4,128)(2,1)S(1)}, u32[]{:S(2)}, u32[]{:S(2)}) collective-permute-start(bf16[18,4,128]{2,1,0:T(4,128)(2,1)S(1)} %broadcast_select_fusion.12), channel_id=1, source_target_pairs={{0,6},{2,8},{4,10},{6,12},{8,14},{10,16},{12,18},{14,20},{16,22},{... | collective-permute-start | bytes 55304 | tf_op jit(solution)/shard_map/ppermute | solution.py:27
  364.5 21.6 %copy-start.23 = (pred[18]{0:T(512)(128)(4,1)S(1)}, pred[18]{0:T(512)(128)(4,1)}, u32[]{:S(2)}) copy-start(pred[18]{0:T(512)(128)(4,1)} %get-tuple-element.105) | copy-start | bytes 58
  364.5 22.3 %copy-start.22 = (pred[18]{0:T(512)(128)(4,1)S(1)}, pred[18]{0:T(512)(128)(4,1)}, u32[]{:S(2)}) copy-start(pred[18]{0:T(512)(128)(4,1)} %get-tuple-element.181) | copy-start | bytes 58
  364.5 22.9 %copy-start.21 = (pred[352]{0:T(512)(128)(4,1)S(1)}, pred[352]{0:T(512)(128)(4,1)}, u32[]{:S(2)}) copy-start(pred[352]{0:T(512)(128)(4,1)} %compare_and_fusion.17) | copy-start | bytes 1060
  365.3 23.3 %copy-start.24 = (pred[18]{0:T(512)(128)(4,1)S(1)}, pred[18]{0:T(512)(128)(4,1)}, u32[]{:S(2)}) copy-start(pred[18]{0:T(512)(128)(4,1)} %get-tuple-element.109) | copy-start | bytes 58
  371.4 17.4 %collective-permute-start.18 = (bf16[17,4,128]{2,1,0:T(4,128)(2,1)}, bf16[17,4,128]{2,1,0:T(4,128)(2,1)}, u32[]{:S(2)}, u32[]{:S(2)}) collective-permute-start(bf16[17,4,128]{2,1,0:T(4,128)(2,1)} %broadcast_select_fusion.21), channel_id=1, source_target_pairs={{0,8},{2,10},{4,12},{6,14},{8,16},{10,18},{12,20},{14,22},{16,24},... | collective-permute-start | bytes 52232 | tf_op jit(solution)/shard_map/ppermute | solution.py:27
  372.1 16.7 %collective-permute-start.25 = (bf16[17,4,128]{2,1,0:T(4,128)(2,1)}, bf16[17,4,128]{2,1,0:T(4,128)(2,1)}, u32[]{:S(2)}, u32[]{:S(2)}) collective-permute-start(bf16[17,4,128]{2,1,0:T(4,128)(2,1)} %broadcast_select_fusion.20), channel_id=1, source_target_pairs={{0,24},{2,26},{4,28},{6,30},{8,0},{10,2},{12,4},{14,6},{16,8},{18,... | collective-permute-start | bytes 52232 | tf_op jit(solution)/shard_map/ppermute | solution.py:27
  376.6 16.9 %collective-permute-start.19 = (bf16[18,4,128]{2,1,0:T(4,128)(2,1)}, bf16[18,4,128]{2,1,0:T(4,128)(2,1)S(1)}, u32[]{:S(2)}, u32[]{:S(2)}) collective-permute-start(bf16[18,4,128]{2,1,0:T(4,128)(2,1)} %broadcast_select_fusion.11), channel_id=1, source_target_pairs={{0,6},{2,8},{4,10},{6,12},{8,14},{10,16},{12,18},{14,20},{16,22},{... | collective-permute-start | bytes 55304 | tf_op jit(solution)/shard_map/ppermute | solution.py:27
  381.2 41.6 %collective-permute-start.21 = (bf16[214,4,128]{2,1,0:T(4,128)(2,1)S(1)}, bf16[214,4,128]{2,1,0:T(4,128)(2,1)S(1)}, u32[]{:S(2)}, u32[]{:S(2)}) collective-permute-start(bf16[214,4,128]{2,1,0:T(4,128)(2,1)S(1)} %broadcast_select_fusion.3), channel_id=1, source_target_pairs={{0,2},{2,4},{4,6},{6,8},{8,10},{10,12},{12,14},{14,16},{16,18},{18... | collective-permute-start | bytes 657416 | tf_op jit(solution)/shard_map/ppermute | solution.py:27
  381.6 49.7 %collective-permute-start.22 = (bf16[214,4,128]{2,1,0:T(4,128)(2,1)S(1)}, bf16[214,4,128]{2,1,0:T(4,128)(2,1)S(1)}, u32[]{:S(2)}, u32[]{:S(2)}) collective-permute-start(bf16[214,4,128]{2,1,0:T(4,128)(2,1)S(1)} %broadcast_select_fusion.2), channel_id=1, source_target_pairs={{0,30},{2,0},{4,2},{6,4},{8,6},{10,8},{12,10},{14,12},{16,14},{18,... | collective-permute-start | bytes 657416 | tf_op jit(solution)/shard_map/ppermute | solution.py:27
  388.7 29.8 %collective-permute-start.20 = (bf16[18,4,128]{2,1,0:T(4,128)(2,1)S(1)}, bf16[18,4,128]{2,1,0:T(4,128)(2,1)S(1)}, u32[]{:S(2)}, u32[]{:S(2)}) collective-permute-start(bf16[18,4,128]{2,1,0:T(4,128)(2,1)S(1)} %broadcast_select_fusion.10), channel_id=1, source_target_pairs={{0,4},{2,6},{4,8},{6,10},{8,12},{10,14},{12,16},{14,18},{16,20},{1... | collective-permute-start | bytes 55304 | tf_op jit(solution)/shard_map/ppermute | solution.py:27
  388.8 33.9 %collective-permute-start.23 = (bf16[18,4,128]{2,1,0:T(4,128)(2,1)}, bf16[18,4,128]{2,1,0:T(4,128)(2,1)S(1)}, u32[]{:S(2)}, u32[]{:S(2)}) collective-permute-start(bf16[18,4,128]{2,1,0:T(4,128)(2,1)} %broadcast_select_fusion.9), channel_id=1, source_target_pairs={{0,28},{2,30},{4,0},{6,2},{8,4},{10,6},{12,8},{14,10},{16,12},{18,... | collective-permute-start | bytes 55304 | tf_op jit(solution)/shard_map/ppermute | solution.py:27
  393.5 29.2 %collective-permute-start.24 = (bf16[18,4,128]{2,1,0:T(4,128)(2,1)}, bf16[18,4,128]{2,1,0:T(4,128)(2,1)S(1)}, u32[]{:S(2)}, u32[]{:S(2)}) collective-permute-start(bf16[18,4,128]{2,1,0:T(4,128)(2,1)} %broadcast_select_fusion.8), channel_id=1, source_target_pairs={{0,26},{2,28},{4,30},{6,0},{8,2},{10,4},{12,6},{14,8},{16,10},{18,... | collective-permute-start | bytes 55304 | tf_op jit(solution)/shard_map/ppermute | solution.py:27
  398.2 22.8 %copy-start.32 = (s32[18]{0:T(128)S(1)}, s32[18]{0:T(128)}, u32[]{:S(2)}) copy-start(s32[18]{0:T(128)} %fusion.27) | copy-start | bytes 220
  398.2 24.7 %copy-start.20 = (s32[214,1]{0,1:T(1,128)S(1)}, s32[214,1]{0,1:T(1,128)}, u32[]{:S(2)}) copy-start(s32[214,1]{0,1:T(1,128)} %compare_select_fusion.4) | copy-start | bytes 2572
  402.8 28.5 %copy-start.19 = (s32[214,1]{0,1:T(1,128)S(1)}, s32[214,1]{0,1:T(1,128)}, u32[]{:S(2)}) copy-start(s32[214,1]{0,1:T(1,128)} %compare_select_fusion.3) | copy-start | bytes 2572
  402.8 36.9 %copy-start.31 = (s32[18]{0:T(128)S(1)}, s32[18]{0:T(128)}, u32[]{:S(2)}) copy-start(s32[18]{0:T(128)} %fusion.28) | copy-start | bytes 220
  402.8 38.6 %copy-start.30 = (s32[18]{0:T(128)S(1)}, s32[18]{0:T(128)}, u32[]{:S(2)}) copy-start(s32[18]{0:T(128)} %fusion.29) | copy-start | bytes 220
  402.8 40.3 %copy-start.35 = (s32[17]{0:T(128)S(1)}, s32[17]{0:T(128)}, u32[]{:S(2)}) copy-start(s32[17]{0:T(128)} %fusion.30) | copy-start | bytes 208
  418.5 26.3 %collective-permute-start.26 = (bf16[1,4,128]{2,1,0:T(4,128)(2,1)S(1)}, bf16[1,4,128]{2,1,0:T(4,128)(2,1)S(1)}, u32[]{:S(2)}, u32[]{:S(2)}) collective-permute-start(bf16[1,4,128]{2,1,0:T(4,128)(2,1)S(1)} %fusion.22), channel_id=1, source_target_pairs={{0,16},{2,18},{4,20},{6,22},{8,24},{10,26},{12,28},{14,30},{16,0},... | collective-permute-start | bytes 3080 | tf_op jit(solution)/shard_map/ppermute | solution.py:27
  458.3 28.6 %slice-start = ((s8[6291456]{0:T(1024)(128)(4,1)}), s8[2097152]{0:T(1024)(128)(4,1)S(1)}, s32[]{:S(2)}) async-start(s8[6291456]{0:T(1024)(128)(4,1)} %bitcast.277), calls=%async_computation.1 | async-start | bytes 4194304
  489.9 149.8 %copy-start.1 = (bf16[3,3,128,128]{3,2,1,0:T(8,128)(2,1)S(1)}, bf16[3,3,128,128]{3,2,1,0:T(8,128)(2,1)}, u32[]{:S(2)}) copy-start(bf16[3,3,128,128]{3,2,1,0:T(8,128)(2,1)} %param.75) | copy-start | bytes 884740
  (23 other events, 195.2 us)
Sparse Core Ops, SparseCore 0:
  503.6 132.1 all-reduce.15
where the time goes:
time: 658 us; the launch traced here: 647 us
  local copies, waits for them, and re-layouts  204 us (31%)
  other arithmetic  161 us (24%)
  waiting for transfers between devices  105 us (16%)
  matrix products  79.2 us (12%)
  blocking collectives  40.2 us (6%)
  starting transfers between devices  38 us (6%)
  between operations  19.6 us (3%)
    psum x1, waiting for transfers between devices, body(): lax.psum((grad_terms[0], grad_terms[1], grad_terms[2], grad_terms[3]), ('...  91.1 us
    unnamed x128, local copies, waits for them, and re-layouts  55.9 us
    psum x1, blocking collectives, body(): lax.psum((grad_terms[0], grad_terms[1], grad_terms[2], grad_terms[3]), ('...  40.2 us
    ppermute x27, starting transfers between devices, passed_along(): return lax.ppermute(value, axis, pairs)  38 us
    squeeze x1, local copies, waits for them, and re-layouts, spread_back(): parts[..., row_off * 3 + col_off, :]  37.5 us
    gather x16, local copies, waits for them, and re-layouts, fill_border(): jnp.take(rim_ext, select_row(forward_rows[position], tile_index), axis=0)  28.3 us
    scatter-add x9, other arithmetic, fold_border(): rim_grad.at[select_row(target_rows[position], tile_index)]  27.5 us
    another operation x2, other arithmetic  24.4 us
  transfers between devices with their start and end apart: 28, of which 5 were waited for; matrix products, arithmetic and copies ran while one was open for 20% of the time, Pallas kernels for 0%

commit v1 on v0

v1 whole, which is shorter than its diff:
```python
import math

import jax
import jax.numpy as jnp
import numpy as np
from jax import lax
from jax.experimental import pallas as pl
from jax.experimental.pallas import tpu as pltpu
from jax.sharding import PartitionSpec as P

S = 4


inv_sqrt_two = 0.7071067811865476
inv_sqrt_tau = 0.3989422804014327


def passed_along(value, axis, steps):
    count = lax.axis_size(axis)
    pairs = [(source, (source + steps) % count) for source in range(count)]
    return lax.ppermute(value, axis, pairs)


def edge_partner(face_id, edge_id):
    group_id = face_id // 4
    within = face_id % 4
    after_id = (within + 1) % 4
    before = (within + 3) % 4
    if group_id == 0:
        options = [(after_id, 2), (4 + within, 0), (before, 0), (4 + after_id, 2)]
    elif group_id == 1:
        options = [(within, 1), (8 + before, 0), (before, 3), (8 + within, 2)]
    else:
        options = [(4 + after_id, 1), (8 + before, 3), (4 + within, 3), (8 + after_id, 1)]
    return options[edge_id]


def entry_pixel(edge_id, along_edge, length):
    if edge_id == 0:
        return (0, along_edge)
    if edge_id == 1:
        return (length - 1, along_edge)
    if edge_id == 2:
        return (along_edge, 0)
    return (along_edge, length - 1)


def step_pixel(face_id, row_at, col_at, row_step, col_step, length):
    row_new = row_at + row_step
    col_new = col_at + col_step
    if 0 <= row_new < length and 0 <= col_new < length:
        return (face_id, row_new, col_new, -1)
    if row_new < 0:
        edge_id = 0
    elif row_new >= length:
        edge_id = 1
    elif col_new < 0:
        edge_id = 2
    else:
        edge_id = 3
    along_edge = col_at if edge_id < 2 else row_at
    partner, entered = edge_partner(face_id, edge_id)
    row_in, col_in = entry_pixel(entered, along_edge, length)
    return (partner, row_in, col_in, entered)


def neighbour_pixel(face_id, row_at, col_at, row_step, col_step, length):
    if row_step == 0 or col_step == 0:
        found = step_pixel(face_id, row_at, col_at, row_step, col_step, length)
        return (found[0], found[1], found[2])
    face_one, row_one, col_one, entered = step_pixel(face_id, row_at, col_at, row_step, 0, length)
    if entered >= 2:
        found = step_pixel(face_one, row_one, col_one, col_step, 0, length)
    else:
        found = step_pixel(face_one, row_one, col_one, 0, col_step, length)
    return (found[0], found[1], found[2])


def tile_slot(face_id, tile_row, tile_col, side_tiles):
    group_id = face_id // 4
    within = face_id % 4
    extra = 1 if group_id == 2 else 0
    column = (side_tiles * (within + extra) + tile_col) % (4 * side_tiles)
    return 3 * side_tiles * column + side_tiles * group_id + tile_row


def cycle_position(row_at, col_at, pixels):
    if row_at == 0:
        return col_at
    if row_at == pixels - 1:
        return pixels + col_at
    if col_at == 0:
        return 2 * pixels + row_at
    return 3 * pixels + row_at


def halo_positions(pixels):
    places = [(-1, column) for column in range(-1, pixels + 1)]
    places = places + [(pixels, column) for column in range(-1, pixels + 1)]
    places = places + [(row_at, -1) for row_at in range(pixels)]
    places = places + [(row_at, pixels) for row_at in range(pixels)]
    return places


def halo_sources(side_tiles, pixels):
    slot_count = 12 * side_tiles * side_tiles
    places = halo_positions(pixels)
    length = side_tiles * pixels
    source_slot = np.zeros((slot_count, len(places)), np.int64)
    source_cycle = np.zeros((slot_count, len(places)), np.int64)
    for face_id in range(12):
        for tile_row in range(side_tiles):
            for tile_col in range(side_tiles):
                slot_id = tile_slot(face_id, tile_row, tile_col, side_tiles)
                for cell_index in range(len(places)):
                    row_at, col_at = places[cell_index]
                    inner_row = min(max(row_at, 0), pixels - 1)
                    inner_col = min(max(col_at, 0), pixels - 1)
                    partner, row_new, col_new = neighbour_pixel(
                        face_id,
                        tile_row * pixels + inner_row,
                        tile_col * pixels + inner_col,
                        row_at - inner_row,
                        col_at - inner_col,
                        length,
                    )
                    source_slot[slot_id, cell_index] = tile_slot(
                        partner, row_new // pixels, col_new // pixels, side_tiles
                    )
                    source_cycle[slot_id, cell_index] = cycle_position(
                        row_new % pixels, col_new % pixels, pixels
                    )
    return (source_slot, source_cycle)


def halo_rows(row_at, col_at, pixels):
    if row_at == -1 or row_at == pixels:
        base = 0 if row_at == -1 else 3 * pixels
        return [
            base + pixels * shift + col_at + 1 - shift
            for shift in range(3)
            if 0 <= col_at + 1 - shift < pixels
        ]
    return [6 * pixels + row_at if col_at == -1 else 7 * pixels + row_at]


def outer_row(row_at, col_at, pixels):
    if col_at == -1:
        return 2 * pixels + row_at + 1
    if col_at == pixels:
        return 4 * pixels + row_at + 1
    return col_at if row_at == -1 else pixels + col_at


def device_tables(device_count, per_device, side_tiles, pixels):
    source_slot, source_cycle = halo_sources(side_tiles, pixels)
    places = halo_positions(pixels)
    rim_len, halo_len, outer_len = 4 * pixels, 8 * pixels, 6 * pixels
    sends = {}
    local = []
    for device in range(device_count):
        local.append([])
        for local_id in range(per_device):
            slot_id = device * per_device + local_id
            for cell in range(len(places)):
                row_at, col_at = places[cell]
                source = int(source_slot[slot_id, cell])
                moved_by = (device - source // per_device) % device_count
                if moved_by > device_count // 2:
                    moved_by -= device_count
                rim = source % per_device * rim_len + int(source_cycle[slot_id, cell])
                halo = [local_id * halo_len + h for h in halo_rows(row_at, col_at, pixels)]
                outer = local_id * outer_len + outer_row(row_at, col_at, pixels)
                record = (rim, halo, outer)
                if moved_by == 0:
                    local[device].append(record)
                else:
                    lists = sends.setdefault(moved_by, [[] for _ in range(device_count)])
                    lists[device].append(record)
    offsets = sorted(sends)
    widths = [-(-max(len(one) for one in sends[offset]) // 16) * 16 for offset in offsets]
    total = sum(widths)
    send = np.full((device_count, total), -1, np.int32)
    receive = np.full((device_count, per_device * halo_len), -1, np.int32)
    back = np.full((device_count, total), -1, np.int32)
    target = np.full((device_count, per_device * outer_len + total), -1, np.int32)
    for device in range(device_count):
        for rim, halo, outer in local[device]:
            receive[device, halo] = rim
            target[device, outer] = rim
        base = 0
        for offset, width in zip(offsets, widths):
            sender = (device - offset) % device_count
            for at, (rim, halo, outer) in enumerate(sends[offset][device]):
                send[sender, base + at] = rim
                receive[device, halo] = per_device * rim_len + base + at
                back[device, base + at] = outer
                target[sender, per_device * outer_len + base + at] = rim
            base += width
    return (offsets, widths, send, receive, back, target)


def one_hot(table_np, tile_index, width):
    row = jnp.asarray(table_np, dtype=jnp.int32)[tile_index]
    return (row[:, None] == lax.broadcasted_iota(jnp.int32, (row.shape[0], width), 1)).astype(
        jnp.bfloat16
    )


def exchanged(rows, offsets, widths, sign):
    pieces, base = [], 0
    for offset, width in zip(offsets, widths):
        pieces.append(passed_along(rows[base : base + width], "tile", sign * offset))
        base += width
    return pieces


def halo_of(rim, layout, tile_index):
    offsets, widths, send, receive = layout[:4]
    outgoing = jnp.dot(one_hot(send, tile_index, rim.shape[0]), rim)
    pool = jnp.concatenate([rim] + exchanged(outgoing, offsets, widths, 1), axis=0)
    return jnp.dot(one_hot(receive, tile_index, pool.shape[0]), pool)


def folded(outer, layout, tile_index, rim_rows):
    offsets, widths, _, _, back, target = layout
    outgoing = jnp.dot(one_hot(back, tile_index, outer.shape[0]), outer)
    pool = jnp.concatenate([outer] + exchanged(outgoing, offsets, widths, -1), axis=0)
    spread = one_hot(target, tile_index, rim_rows)
    return lax.dot_general(
        spread, pool, (((0,), (0,)), ((), ())), preferred_element_type=jnp.float32
    )


def gelu_parts(value):
    half = 0.5 * (1.0 + lax.erf(value * inv_sqrt_two))
    return value * half, half + value * jnp.exp(-0.5 * value * value) * inv_sqrt_tau


def columns_at(tile, halo, work, pixels):
    count = pixels * pixels
    wide = tile.astype(jnp.float32)
    halo_wide = halo[6 * pixels :].astype(jnp.float32)
    work[0, pl.ds(1, count - 1), :] = wide[: count - 1]
    work[0, pl.ds(0, pixels, stride=pixels), :] = halo_wide[:pixels]
    work[1, pl.ds(0, count - 1), :] = wide[1:]
    work[1, pl.ds(pixels - 1, pixels, stride=pixels), :] = halo_wide[pixels:]
    middles = [work[0].astype(jnp.bfloat16), tile, work[1].astype(jnp.bfloat16)]
    joined = jnp.concatenate(
        [
            jnp.concatenate(
                [
                    halo[pixels * b : pixels * (b + 1)],
                    middles[b],
                    halo[pixels * (3 + b) : pixels * (4 + b)],
                ],
                axis=0,
            )
            for b in range(3)
        ],
        axis=1,
    )
    return jnp.concatenate([joined[pixels * a : pixels * a + count] for a in range(3)], axis=1)


def first_kernel(x_ref, halo_ref, w_ref, bias_ref, hidden_ref, slope_ref, rim_ref, work):
    batch, pixels, channels = x_ref.shape[1], x_ref.shape[2], x_ref.shape[4]
    count = pixels * pixels
    for s in range(batch):
        lanes = slice(s * channels, (s + 1) * channels)
        tile = x_ref[0, s].reshape(count, channels)
        cols = columns_at(tile, halo_ref[0, :, lanes], work.at[pl.ds(2 * s, 2)], pixels)
        pre = jnp.dot(cols, w_ref[...], preferred_element_type=jnp.float32) + bias_ref[...]
        hidden, slope = gelu_parts(pre)
        slope_ref[0, s] = slope
        work[2 * batch + s] = hidden
        rounded = hidden.astype(jnp.bfloat16)
        hidden_ref[0, s] = rounded.reshape(pixels, pixels, channels)
        rim_ref[0, 0:pixels, lanes] = rounded[:pixels]
        rim_ref[0, pixels : 2 * pixels, lanes] = rounded[count - pixels :]
        for side in range(2):
            edge = work[2 * batch + s, pl.ds(side * (pixels - 1), pixels, stride=pixels), :]
            rim_ref[0, (2 + side) * pixels : (3 + side) * pixels, lanes] = edge.astype(jnp.bfloat16)


def second_kernel(
    x_ref, halo_ref, cot_ref, w_ref, flip_ref, side_ref, bias_ref,
    out_ref, inner_ref, outer_ref, grad_ref, sum_ref, work, cols_ref, delta_ref, edge_ref,
):
    batch, pixels, channels = x_ref.shape[1], x_ref.shape[2], x_ref.shape[4]
    count = pixels * pixels

    @pl.when(pl.program_id(0) == 0)
    def _():
        grad_ref[...] = jnp.zeros_like(grad_ref)
        sum_ref[...] = jnp.zeros_like(sum_ref)

    zero_row = jnp.zeros((1, channels), jnp.float32)
    zero_col = jnp.zeros((pixels, channels), jnp.float32)
    zeros = jnp.zeros((2 * pixels, 3 * channels), jnp.bfloat16)
    for s in range(batch):
        lanes = slice(s * channels, (s + 1) * channels)
        tile = x_ref[0, s].reshape(count, channels)
        here = work.at[pl.ds(2 * s, 2)]
        cols = columns_at(tile, halo_ref[0, :, lanes], here, pixels)
        cols_ref[s * count : (s + 1) * count, :] = cols
        pre = jnp.dot(cols, w_ref[...], preferred_element_type=jnp.float32) + bias_ref[...]
        value, slope = gelu_parts(pre)
        out_ref[0, s] = value.astype(jnp.bfloat16).reshape(pixels, pixels, channels)
        cot = cot_ref[0, s].reshape(count, channels).astype(jnp.float32)
        delta = (cot * slope).astype(jnp.bfloat16)
        delta_ref[s * count : (s + 1) * count, :] = delta
        wide = delta.astype(jnp.float32)
        sum_ref[...] += jnp.sum(wide, axis=0, keepdims=True)
        edge_ref[s] = jnp.zeros(edge_ref.shape[1:], jnp.float32)
        work[2 * batch + s] = wide
        for side in range(2):
            edge_ref[s, side, pl.ds(2, pixels), :] = work[
                2 * batch + s, pl.ds(side * (pixels - 1), pixels, stride=pixels), :
            ]
        here[0, pl.ds(0, count - 1), :] = wide[1:]
        here[0, pl.ds(pixels - 1, pixels, stride=pixels), :] = zero_col
        here[1, pl.ds(1, count - 1), :] = wide[: count - 1]
        here[1, pl.ds(0, pixels, stride=pixels), :] = zero_col
        joined = jnp.concatenate(
            [here[0].astype(jnp.bfloat16), delta, here[1].astype(jnp.bfloat16)], axis=1
        )
        joined = jnp.concatenate([zeros, joined, zeros], axis=0)
        tall = count + 2 * pixels
        spread = jnp.concatenate(
            [joined[pixels * (2 - a) : pixels * (2 - a) + tall] for a in range(3)], axis=1
        )
        grad = jnp.dot(spread, flip_ref[...], preferred_element_type=jnp.float32)
        inner_ref[0, s] = grad[pixels : pixels + count]
        outer_ref[0, 0:pixels, lanes] = grad[:pixels].astype(jnp.bfloat16)
        outer_ref[0, pixels : 2 * pixels, lanes] = grad[pixels + count :].astype(jnp.bfloat16)
        for side in range(2):
            lhs = jnp.concatenate(
                [edge_ref[s, side, pl.ds(2 - a, 2 * pixels), :] for a in range(3)], axis=1
            ).astype(jnp.bfloat16)
            part = jnp.dot(lhs, side_ref[side], preferred_element_type=jnp.float32)
            outer_ref[0, 2 * pixels * (1 + side) : 2 * pixels * (2 + side), lanes] = part.astype(
                jnp.bfloat16
            )
    grad_ref[...] += lax.dot_general(
        delta_ref[...], cols_ref[...], (((0,), (0,)), ((), ())), preferred_element_type=jnp.float32
    )


def third_kernel(
    x_ref, halo_ref, inner_ref, rim_ref, slope_ref, grad_ref, sum_ref, work, cols_ref, delta_ref
):
    batch, pixels, channels = x_ref.shape[1], x_ref.shape[2], x_ref.shape[4]
    count = pixels * pixels

    @pl.when(pl.program_id(0) == 0)
    def _():
        grad_ref[...] = jnp.zeros_like(grad_ref)
        sum_ref[...] = jnp.zeros_like(sum_ref)

    for s in range(batch):
        lanes = slice(s * channels, (s + 1) * channels)
        tile = x_ref[0, s].reshape(count, channels)
        cols_ref[s * count : (s + 1) * count, :] = columns_at(
            tile, halo_ref[0, :, lanes], work.at[pl.ds(2 * s, 2)], pixels
        )
        at = 2 * batch + s
        work[at] = inner_ref[0, s]
        work[at, pl.ds(0, pixels), :] += rim_ref[0, 0:pixels, lanes]
        work[at, pl.ds(count - pixels, pixels), :] += rim_ref[0, pixels : 2 * pixels, lanes]
        for side in range(2):
            place = pl.ds(side * (pixels - 1), pixels, stride=pixels)
            edge = rim_ref[0, (2 + side) * pixels : (3 + side) * pixels, lanes]
            work[at, place, :] = work[at, place, :] + edge
        delta = (work[at] * slope_ref[0, s]).astype(jnp.bfloat16)
        delta_ref[s * count : (s + 1) * count, :] = delta
        sum_ref[...] += jnp.sum(delta.astype(jnp.float32), axis=0, keepdims=True)
    grad_ref[...] += lax.dot_general(
        delta_ref[...], cols_ref[...], (((0,), (0,)), ((), ())), preferred_element_type=jnp.float32
    )


def per_tile(shape):
    return pl.BlockSpec((1,) + tuple(shape), lambda t: (t,) + (0,) * len(shape))


def whole(shape):
    return pl.BlockSpec(tuple(shape), lambda t: (0,) * len(shape))


params = dict(vmem_limit_bytes=48 * 1024 * 1024)


def body(features, weight_one, bias_one, weight_two, bias_two, cotangent):
    device_count = lax.axis_size("tile")
    samples_count = lax.axis_size("tm")
    tile_index = lax.axis_index("tile")
    per_device, batch, pixels, _, channels = features.shape
    count = pixels * pixels
    lane_count = batch * channels
    layout = device_tables(device_count, per_device, S, pixels)
    bf16, f32 = jnp.bfloat16, jnp.float32
    tile_shape = (batch, pixels, pixels, channels)
    flat_shape = (batch, count, channels)
    halo_shape = (8 * pixels, lane_count)
    rim_shape = (4 * pixels, lane_count)
    outer_shape = (6 * pixels, lane_count)
    mat_one = weight_one.reshape(9 * channels, channels)
    mat_two = weight_two.reshape(9 * channels, channels)
    turned = weight_two.transpose(0, 1, 3, 2)
    flip = turned.reshape(9 * channels, channels)
    sides = jnp.stack([turned[:, 0], turned[:, 2]]).reshape(2, 3 * channels, channels)

    def out(shape, dtype):
        return jax.ShapeDtypeStruct((per_device,) + tuple(shape), dtype)

    work = pltpu.VMEM((3 * batch, count, channels), f32)
    cols = pltpu.VMEM((batch * count, 9 * channels), bf16)
    deltas = pltpu.VMEM((batch * count, channels), bf16)
    grad_shape = (channels, 9 * channels)

    rim_one = jnp.concatenate(
        [features[:, :, 0], features[:, :, -1], features[:, :, :, 0], features[:, :, :, -1]], axis=2
    )
    rim_one = rim_one.transpose(0, 2, 1, 3).reshape(per_device * 4 * pixels, lane_count)
    halo_one = halo_of(rim_one, layout, tile_index).reshape((per_device,) + halo_shape)
    hidden, slope, rim_two = pl.pallas_call(
        first_kernel,
        grid=(per_device,),
        in_specs=[per_tile(tile_shape), per_tile(halo_shape), whole(mat_one.shape), whole((1, channels))],
        out_specs=[per_tile(tile_shape), per_tile(flat_shape), per_tile(rim_shape)],
        out_shape=[out(tile_shape, bf16), out(flat_shape, f32), out(rim_shape, bf16)],
        scratch_shapes=[work],
        compiler_params=pltpu.CompilerParams(**params),
    )(features, halo_one, mat_one, bias_one.reshape(1, channels))
    halo_two = halo_of(rim_two.reshape(-1, lane_count), layout, tile_index)
    output, inner, outer, grad_two, sum_two = pl.pallas_call(
        second_kernel,
        grid=(per_device,),
        in_specs=[
            per_tile(tile_shape), per_tile(halo_shape), per_tile(tile_shape), whole(mat_two.shape),
            whole(flip.shape), whole(sides.shape), whole((1, channels)),
        ],
        out_specs=[
            per_tile(tile_shape), per_tile(flat_shape), per_tile(outer_shape),
            whole(grad_shape), whole((1, channels)),
        ],
        out_shape=[
            out(tile_shape, bf16), out(flat_shape, f32), out(outer_shape, bf16),
            jax.ShapeDtypeStruct(grad_shape, f32), jax.ShapeDtypeStruct((1, channels), f32),
        ],
        scratch_shapes=[work, cols, deltas, pltpu.VMEM((batch, 2, 2 * pixels + 8, channels), f32)],
        compiler_params=pltpu.CompilerParams(**params),
    )(
        hidden, halo_two.reshape((per_device,) + halo_shape), cotangent, mat_two, flip, sides,
        bias_two.reshape(1, channels),
    )
    rim_grad = folded(outer.reshape(-1, lane_count), layout, tile_index, per_device * 4 * pixels)
    grad_one, sum_one = pl.pallas_call(
        third_kernel,
        grid=(per_device,),
        in_specs=[
            per_tile(tile_shape), per_tile(halo_shape), per_tile(flat_shape), per_tile(rim_shape),
            per_tile(flat_shape),
        ],
        out_specs=[whole(grad_shape), whole((1, channels))],
        out_shape=[jax.ShapeDtypeStruct(grad_shape, f32), jax.ShapeDtypeStruct((1, channels), f32)],
        scratch_shapes=[work, cols, deltas],
        compiler_params=pltpu.CompilerParams(**params),
    )(features, halo_one, inner, rim_grad.reshape((per_device,) + rim_shape), slope)

    total_pixels = 12 * S * S * count * batch * samples_count
    grad_scale = 1.0 / math.sqrt(total_pixels)
    devices = device_count * samples_count
    axes = ("tile", "tm")

    def summed(grad, bias):
        rows = jnp.concatenate([grad.reshape(-1, channels), bias], axis=0)
        used = rows.shape[0]
        chunk = -(-used // (8 * devices)) * 8
        rows = jnp.pad(rows, ((0, chunk * devices - used), (0, 0)))
        parts = lax.all_to_all(rows.reshape(devices, chunk, channels), axes, 0, 0)
        mine = jnp.sum(parts, axis=0) * grad_scale
        total = lax.all_gather(mine, axes, axis=0, tiled=True)
        weight = total[: used - 1].reshape(channels, 3, 3, channels).transpose(1, 2, 3, 0)
        return weight, total[used - 1]

    grad_weight_two, grad_bias_two = summed(grad_two, sum_two)
    grad_weight_one, grad_bias_one = summed(grad_one, sum_one)
    return (output, grad_weight_one, grad_bias_one, grad_weight_two, grad_bias_two)


def solution(mesh):
    return jax.shard_map(
        body,
        mesh=mesh,
        in_specs=(
            P("tile", "tm", None, None, None),
            P(),
            P(),
            P(),
            P(),
            P("tile", "tm", None, None, None),
        ),
        out_specs=(P("tile", "tm", None, None, None), P(), P(), P(), P()),
        check_vma=False,
    )
```

time: 658 us -> 317 us (0.48); the launches traced: 647 us -> 316 us
  local copies, waits for them, and re-layouts: 204 us -> 27.8 us
  other arithmetic: 161 us -> 2 us
  blocking collectives: 40.2 us -> 146 us
  waiting for transfers between devices: 105 us -> 12.9 us
  matrix products: 79.2 us -> 13.2 us
  Pallas kernels: 0 us -> 62.1 us
  between operations: 19.6 us -> 1.06 us
  starting transfers between devices: 38 us -> 50.2 us
    all_gather x0 -> x2, blocking collectives: none -> 146 us  [summed(): total = lax.all_gather(mine, axes, axis=0, tiled=True)]
    psum x1 -> x0, waiting for transfers between devices: 91.1 us -> none  [body(): lax.psum((grad_terms[0], grad_terms[1], grad_terms[2], grad_terms[3]), ('...]
    dot_general x5 -> x6, matrix products: 79.2 us -> 13.2 us  [the longest x2 6.96 us: halo_of(): return jnp.dot(one_hot(receive, tile_index, pool.shape[0]), pool)]
    pallas_call x0 -> x3, Pallas kernels: none -> 62.1 us  [the longest x1 34.6 us: body(): pl.pallas_call(second_kernel, grid=(per_device,), in_specs=[per_tile(tile...]
    gather x27 -> x0, local copies, waits for them, and re-layouts: 45.4 us -> none  [the longest x16 28.3 us: fill_border(): jnp.take(rim_ext, select_row(forward_rows[position], tile_index), axis=0)]
    scatter-add x10 -> x0, other arithmetic: 40.6 us -> none  [the longest x9 27.5 us: fold_border(): rim_grad.at[select_row(target_rows[position], tile_index)]]
    psum x1 -> x0, blocking collectives: 40.2 us -> none  [body(): lax.psum((grad_terms[0], grad_terms[1], grad_terms[2], grad_terms[3]), ('...]
    unnamed x128 -> x41, local copies, waits for them, and re-layouts: 55.9 us -> 16.3 us
  transfers between devices with their start and end apart: 28 -> 29, of which waited for: 5 -> 4; matrix products, arithmetic and copies ran while one was open for 20% -> 7% of each run, Pallas kernels for 0% -> 4%
where the time goes in v1:
time: 317 us; the launch traced here: 316 us
  blocking collectives  146 us (46%)
  Pallas kernels  62.1 us (20%)
  starting transfers between devices  50.2 us (16%)
  local copies, waits for them, and re-layouts  27.8 us (9%)
  matrix products  13.2 us (4%)
  waiting for transfers between devices  12.9 us (4%)
    all_gather x2, blocking collectives, summed(): total = lax.all_gather(mine, axes, axis=0, tiled=True)  146 us
    ppermute x27, starting transfers between devices, passed_along(): return lax.ppermute(value, axis, pairs)  39.6 us
    pallas_call x1, Pallas kernels, body(): pl.pallas_call(second_kernel, grid=(per_device,), in_specs=[per_tile(tile...  34.6 us
    unnamed x41, local copies, waits for them, and re-layouts  16.3 us
    pallas_call x1, Pallas kernels, body(): pl.pallas_call(first_kernel, grid=(per_device,), in_specs=[per_tile(tile_...  14 us
    pallas_call x1, Pallas kernels, body(): pl.pallas_call(third_kernel, grid=(per_device,), in_specs=[per_tile(tile_...  13.5 us
    ppermute x27, waiting for transfers between devices, passed_along(): return lax.ppermute(value, axis, pairs)  12.9 us
    all_to_all x2, starting transfers between devices, summed(): parts = lax.all_to_all(rows.reshape(devices, chunk, channels), axes, 0, 0)  10.6 us
  transfers between devices with their start and end apart: 29, of which 4 were waited for; matrix products, arithmetic and copies ran while one was open for 7% of the time, Pallas kernels for 4%

profile of v1, /device:TPU:0, one launch (start us, length us, event | category | flops | bytes accessed | tf_op | source)
XLA Modules:
  0.0 315.5 jit_solution(4220576954632614238)
XLA Ops:
  0.6 2.7 fusion.14
  3.3 1.1 slice_bitcast_fusion.1
  5.2 0.8 dynamic-slice_reduce_fusion.2
  6.0 0.7 fusion.8
  6.8 5.1 %collective-permute-start = (bf16[32,512]{1,0:T(8,128)(2,1)S(1)}, bf16[32,512]{1,0:T(8,128)(2,1)S(1)}, u32[]{:S(2)}, u32[]{:S(2)}) collective-permute-start(bf16[32,512]{1,0:T(8,128)(2,1)S(1)} %get-tuple-element.55), channel_id=1, source_target_pairs={{0,24},{2,26},{4,28},{6,30},{8,0},{10,2},{12,4},{14,6},{16,8},{18,... | collective-permute-start | bytes 98312 | tf_op jit(solution)/shard_map/ppermute | solution.py:21
  11.9 1.4 collective-permute-start.2
  13.3 1.4 collective-permute-start.3
  14.7 1.0 bitcast_dynamic-update-slice_fusion
  16.2 0.8 dynamic-slice_reduce_fusion.1
  17.0 0.9 dynamic-slice_reduce_fusion
  19.2 2.5 collective-permute-start.6
  22.3 1.2 collective-permute-start.7
  24.2 1.6 collective-permute-start.8
  29.7 4.2 %fusion.1 = bf16[1536,512]{1,0:T(8,128)(2,1)S(1)} fusion(bf16[1424,512]{1,0:T(8,128)(2,1)} %constant_dynamic-update-slice_fusion, s32[1536]{0:T(1024)S(1)} %dynamic-slice_reduce_fusion.1), kind=kOutput, calls=%fused_computation.2 | convolution fusion | flops 2241945600 | bytes 3037184 | tf_op jit(solution)/shard_map/dot_general | solution.py:222
  33.9 14.0 %shard_map.155 = (bf16[12,4,16,16,128]{4,3,2,1,0:T(8,128)(2,1)S(1)}, f32[12,4,256,128]{3,2,1,0:T(8,128)}, bf16[12,64,512]{2,1,0:T(8,128)(2,1)S(1)}) custom-call(bf16[12,4,16,16,128]{4,3,2,1,0:T(8,128)(2,1)} %x_ref.3, bf16[12,128,512]{2,1,0:T(8,128)(2,1)S(1)} %bitcast.46, bf16[1152,128]{1,0:T(8,128)(2,1)S(1)} %bitcast.58, f32[1,128]{1,0:T(1,128)S(1)} %bitcast.60), custom_call_target="tpu_custom_call" | custom-call | tf_op jit(solution)/shard_map/pallas_call | solution.py:427
  47.8 0.7 fusion.7
  48.6 0.9 copy-done
  49.5 2.5 collective-permute-start.9
  52.1 2.3 collective-permute-start.11
  54.4 2.5 collective-permute-start.12
  57.0 1.7 collective-permute-start.15
  58.7 1.5 collective-permute-start.16
  60.2 0.9 collective-permute-done.12
  61.0 1.6 collective-permute-start.17
  62.6 3.2 %collective-permute-done.13 = bf16[224,512]{1,0:T(8,128)(2,1)S(1)} collective-permute-done((bf16[224,512]{1,0:T(8,128)(2,1)S(1)}, bf16[224,512]{1,0:T(8,128)(2,1)S(1)}, u32[]{:S(2)}, u32[]{:S(2)}) %collective-permute-start.13) | collective-permute-done | bytes 229408 | tf_op jit(solution)/shard_map/ppermute | solution.py:21
  66.0 2.8 fusion
  68.8 34.6 %shard_map.156 = (bf16[12,4,16,16,128]{4,3,2,1,0:T(8,128)(2,1)}, f32[12,4,256,128]{3,2,1,0:T(8,128)}, bf16[12,96,512]{2,1,0:T(8,128)(2,1)S(1)}, f32[128,1152]{1,0:T(8,128)S(1)}, f32[1,128]{1,0:T(1,128)S(1)}) custom-call(bf16[12,4,16,16,128]{4,3,2,1,0:T(8,128)(2,1)} %copy-done, bf16[12,128,512]{2,1,0:T(8,128)(2,1)S(1)} %bitcast.52, ...), custom_call_target="tpu_custom_call" | custom-call | tf_op jit(solution)/shard_map/pallas_call | solution.py:437
  103.3 0.8 copy-done.2
  104.1 1.1 reshape.86
  105.2 1.1 constant_dynamic-update-slice_fusion.28
  106.3 1.1 fusion.5
  107.5 0.9 select_maximum_fusion
  108.4 6.9 %all-to-all-start.1 = ((f32[32,40,128]{2,1,0:T(8,128)}), f32[32,40,128]{2,1,0:T(8,128)S(1)}, u32[]{:S(2)}, u32[]{:S(2)}) async-start(f32[32,40,128]{2,1,0:T(8,128)} %bitcast.21), calls=%async_computation.1 | async-start | bytes 1310720 | tf_op jit(solution)/shard_map/all_to_all | solution.py:482
  115.3 1.6 collective-permute-start.19
  116.9 1.5 collective-permute-start.20
  118.4 4.4 %collective-permute-start.22 = (bf16[224,512]{1,0:T(8,128)(2,1)S(1)}, bf16[224,512]{1,0:T(8,128)(2,1)S(1)}, u32[]{:S(2)}, u32[]{:S(2)}) collective-permute-start(bf16[224,512]{1,0:T(8,128)(2,1)S(1)} %get-tuple-element.40), channel_id=1, source_target_pairs={{0,30},{2,0},{4,2},{6,4},{8,6},{10,8},{12,10},{14,12},{16,14},{18,... | collective-permute-start | bytes 688136 | tf_op jit(solution)/shard_map/ppermute | solution.py:21
  124.0 6.8 %collective-permute-done.19 = bf16[32,512]{1,0:T(8,128)(2,1)S(1)} collective-permute-done((bf16[32,512]{1,0:T(8,128)(2,1)S(1)}, bf16[32,512]{1,0:T(8,128)(2,1)S(1)}, u32[]{:S(2)}, u32[]{:S(2)}) %collective-permute-start.19) | collective-permute-done | bytes 32800 | tf_op jit(solution)/shard_map/ppermute | solution.py:21
  131.4 2.0 collective-permute-done.20
  133.4 3.8 %collective-permute-start.25 = (bf16[32,512]{1,0:T(8,128)(2,1)S(1)}, bf16[32,512]{1,0:T(8,128)(2,1)S(1)}, u32[]{:S(2)}, u32[]{:S(2)}) collective-permute-start(bf16[32,512]{1,0:T(8,128)(2,1)S(1)} %get-tuple-element.34), channel_id=1, source_target_pairs={{0,24},{2,26},{4,28},{6,30},{8,0},{10,2},{12,4},{14,6},{16,8},{18,... | collective-permute-start | bytes 98312 | tf_op jit(solution)/shard_map/ppermute | solution.py:21
  137.8 1.7 collective-permute-start.26
  143.4 3.7 %fusion.2 = f32[768,512]{1,0:T(8,128)S(1)} fusion(bf16[1808,512]{1,0:T(8,128)(2,1)} %constant_dynamic-update-slice_fusion.19, s32[1808]{0:T(1024)S(1)} %dynamic-slice_reduce_fusion), kind=kOutput, calls=%fused_computation.4 | convolution fusion | flops 1423257600 | bytes 3431488 | tf_op jit(solution)/shard_map/dot_general | solution.py:230
  147.0 13.5 %shard_map.157 = (f32[128,1152]{1,0:T(8,128)S(1)}, f32[1,128]{1,0:T(1,128)S(1)}) custom-call(bf16[12,4,16,16,128]{4,3,2,1,0:T(8,128)(2,1)} %x_ref.3, bf16[12,128,512]{2,1,0:T(8,128)(2,1)S(1)} %bitcast.47, f32[12,4,256,128]{3,2,1,0:T(8,128)} %get-tuple-element.18.inner_ref, f32[12,64,512]{2,1,0:T(8,128)S(1)} %bitcast.51, ...), custom_call_target="tpu_custom_call" | custom-call | tf_op jit(solution)/shard_map/pallas_call | solution.py:459
  160.6 0.9 select_maximum_fusion.1
  161.5 3.7 %all-to-all-start = ((f32[32,40,128]{2,1,0:T(8,128)}), f32[32,40,128]{2,1,0:T(8,128)S(1)}, u32[]{:S(2)}, u32[]{:S(2)}) async-start(f32[32,40,128]{2,1,0:T(8,128)} %bitcast.18), calls=%async_computation | async-start | bytes 1310720 | tf_op jit(solution)/shard_map/all_to_all | solution.py:482
  165.3 76.5 %all_gather.7 = f32[1280,128]{1,0:T(8,128)S(1)} all-gather(f32[40,128]{1,0:T(8,128)S(1)} %broadcast_multiply_fusion), channel_id=1, replica_groups=mesh['tile'=16,'tm'=2] {'tile','tm'}, dimensions={0}, use_global_device_ids=true | all-gather | bytes 675840 | tf_op jit(solution)/shard_map/all_gather | solution.py:484
  242.1 1.1 copy.32
  243.8 69.8 %all_gather.6 = f32[1280,128]{1,0:T(8,128)S(1)} all-gather(f32[40,128]{1,0:T(8,128)S(1)} %broadcast_multiply_fusion.1), channel_id=1, replica_groups=mesh['tile'=16,'tm'=2] {'tile','tm'}, dimensions={0}, use_global_device_ids=true | all-gather | bytes 675840 | tf_op jit(solution)/shard_map/all_gather | solution.py:484
  314.4 1.1 copy.31
  (101 shorter events, 16.2 us)
Async XLA Ops:
  6.7 9.0 %copy-start.1 = (bf16[3,3,128,128]{3,2,1,0:T(8,128)(2,1)S(1)}, bf16[3,3,128,128]{3,2,1,0:T(8,128)(2,1)}, u32[]{:S(2)}) copy-start(bf16[3,3,128,128]{3,2,1,0:T(8,128)(2,1)} %param.15) | copy-start | bytes 884740
  6.8 11.2 %collective-permute-start = (bf16[32,512]{1,0:T(8,128)(2,1)S(1)}, bf16[32,512]{1,0:T(8,128)(2,1)S(1)}, u32[]{:S(2)}, u32[]{:S(2)}) collective-permute-start(bf16[32,512]{1,0:T(8,128)(2,1)S(1)} %get-tuple-element.55), channel_id=1, source_target_pairs={{0,24},{2,26},{4,28},{6,30},{8,0},{10,2},{12,4},{14,6},{16,8},{18,... | collective-permute-start | bytes 98312 | tf_op jit(solution)/shard_map/ppermute | solution.py:21
  11.9 7.4 %collective-permute-start.1 = (bf16[32,512]{1,0:T(8,128)(2,1)S(1)}, bf16[32,512]{1,0:T(8,128)(2,1)S(1)}, u32[]{:S(2)}, u32[]{:S(2)}) collective-permute-start(bf16[32,512]{1,0:T(8,128)(2,1)S(1)} %get-tuple-element.54), channel_id=1, source_target_pairs={{0,26},{2,28},{4,30},{6,0},{8,2},{10,4},{12,6},{14,8},{16,10},{18,... | collective-permute-start | bytes 98312 | tf_op jit(solution)/shard_map/ppermute | solution.py:21
  11.9 10.5 %collective-permute-start.2 = (bf16[32,512]{1,0:T(8,128)(2,1)S(1)}, bf16[32,512]{1,0:T(8,128)(2,1)S(1)}, u32[]{:S(2)}, u32[]{:S(2)}) collective-permute-start(bf16[32,512]{1,0:T(8,128)(2,1)S(1)} %get-tuple-element.53), channel_id=1, source_target_pairs={{0,28},{2,30},{4,0},{6,2},{8,4},{10,6},{12,8},{14,10},{16,12},{18,... | collective-permute-start | bytes 98312 | tf_op jit(solution)/shard_map/ppermute | solution.py:21
  13.3 10.9 %collective-permute-start.3 = (bf16[224,512]{1,0:T(8,128)(2,1)S(1)}, bf16[224,512]{1,0:T(8,128)(2,1)S(1)}, u32[]{:S(2)}, u32[]{:S(2)}) collective-permute-start(bf16[224,512]{1,0:T(8,128)(2,1)S(1)} %get-tuple-element.57), channel_id=1, source_target_pairs={{0,30},{2,0},{4,2},{6,4},{8,6},{10,8},{12,10},{14,12},{16,14},{18,... | collective-permute-start | bytes 688136 | tf_op jit(solution)/shard_map/ppermute | solution.py:21
  14.7 11.8 %collective-permute-start.4 = (bf16[224,512]{1,0:T(8,128)(2,1)S(1)}, bf16[224,512]{1,0:T(8,128)(2,1)S(1)}, u32[]{:S(2)}, u32[]{:S(2)}) collective-permute-start(bf16[224,512]{1,0:T(8,128)(2,1)S(1)} %get-tuple-element.56), channel_id=1, source_target_pairs={{0,2},{2,4},{4,6},{6,8},{8,10},{10,12},{12,14},{14,16},{16,18},{18... | collective-permute-start | bytes 688136 | tf_op jit(solution)/shard_map/ppermute | solution.py:21
  17.9 9.3 %collective-permute-start.5 = (bf16[32,512]{1,0:T(8,128)(2,1)S(1)}, bf16[32,512]{1,0:T(8,128)(2,1)S(1)}, u32[]{:S(2)}, u32[]{:S(2)}) collective-permute-start(bf16[32,512]{1,0:T(8,128)(2,1)S(1)} %get-tuple-element.52), channel_id=1, source_target_pairs={{0,4},{2,6},{4,8},{6,10},{8,12},{10,14},{12,16},{14,18},{16,20},{1... | collective-permute-start | bytes 98312 | tf_op jit(solution)/shard_map/ppermute | solution.py:21
  19.2 8.6 %collective-permute-start.6 = (bf16[32,512]{1,0:T(8,128)(2,1)S(1)}, bf16[32,512]{1,0:T(8,128)(2,1)S(1)}, u32[]{:S(2)}, u32[]{:S(2)}) collective-permute-start(bf16[32,512]{1,0:T(8,128)(2,1)S(1)} %get-tuple-element.51), channel_id=1, source_target_pairs={{0,6},{2,8},{4,10},{6,12},{8,14},{10,16},{12,18},{14,20},{16,22},{... | collective-permute-start | bytes 98312 | tf_op jit(solution)/shard_map/ppermute | solution.py:21
  22.3 6.1 %collective-permute-start.7 = (bf16[32,512]{1,0:T(8,128)(2,1)S(1)}, bf16[32,512]{1,0:T(8,128)(2,1)S(1)}, u32[]{:S(2)}, u32[]{:S(2)}) collective-permute-start(bf16[32,512]{1,0:T(8,128)(2,1)S(1)} %get-tuple-element.50), channel_id=1, source_target_pairs={{0,8},{2,10},{4,12},{6,14},{8,16},{10,18},{12,20},{14,22},{16,24},... | collective-permute-start | bytes 98312 | tf_op jit(solution)/shard_map/ppermute | solution.py:21
  24.2 4.9 %collective-permute-start.8 = (bf16[16,512]{1,0:T(8,128)(2,1)S(1)}, bf16[16,512]{1,0:T(8,128)(2,1)S(1)}, u32[]{:S(2)}, u32[]{:S(2)}) collective-permute-start(bf16[16,512]{1,0:T(8,128)(2,1)S(1)} %slice.156), channel_id=1, source_target_pairs={{0,16},{2,18},{4,20},{6,22},{8,24},{10,26},{12,28},{14,30},{16,0},... | collective-permute-start | bytes 49160 | tf_op jit(solution)/shard_map/ppermute | solution.py:21
  29.7 4.2 %copy-start.3 = (bf16[3,3,128,128]{3,2,1,0:T(8,128)(2,1)S(1)}, bf16[3,3,128,128]{3,2,1,0:T(8,128)(2,1)}, u32[]{:S(2)}) copy-start(bf16[3,3,128,128]{3,2,1,0:T(8,128)(2,1)} %param.13) | copy-start | bytes 884740
  29.7 4.2 %copy-start.5 = (f32[128]{0:T(128)S(1)}, f32[128]{0:T(128)}, u32[]{:S(2)}) copy-start(f32[128]{0:T(128)} %param.14) | copy-start | bytes 1540
  47.8 1.6 copy-start
  49.5 7.4 %collective-permute-start.9 = (bf16[32,512]{1,0:T(8,128)(2,1)S(1)}, bf16[32,512]{1,0:T(8,128)(2,1)S(1)}, u32[]{:S(2)}, u32[]{:S(2)}) collective-permute-start(bf16[32,512]{1,0:T(8,128)(2,1)S(1)} %get-tuple-element.47), channel_id=1, source_target_pairs={{0,24},{2,26},{4,28},{6,30},{8,0},{10,2},{12,4},{14,6},{16,8},{18,... | collective-permute-start | bytes 98312 | tf_op jit(solution)/shard_map/ppermute | solution.py:21
  52.1 4.9 %collective-permute-start.10 = (bf16[32,512]{1,0:T(8,128)(2,1)S(1)}, bf16[32,512]{1,0:T(8,128)(2,1)S(1)}, u32[]{:S(2)}, u32[]{:S(2)}) collective-permute-start(bf16[32,512]{1,0:T(8,128)(2,1)S(1)} %get-tuple-element.46), channel_id=1, source_target_pairs={{0,26},{2,28},{4,30},{6,0},{8,2},{10,4},{12,6},{14,8},{16,10},{18,... | collective-permute-start | bytes 98312 | tf_op jit(solution)/shard_map/ppermute | solution.py:21
  52.1 6.5 %collective-permute-start.11 = (bf16[32,512]{1,0:T(8,128)(2,1)S(1)}, bf16[32,512]{1,0:T(8,128)(2,1)S(1)}, u32[]{:S(2)}, u32[]{:S(2)}) collective-permute-start(bf16[32,512]{1,0:T(8,128)(2,1)S(1)} %get-tuple-element.45), channel_id=1, source_target_pairs={{0,28},{2,30},{4,0},{6,2},{8,4},{10,6},{12,8},{14,10},{16,12},{18,... | collective-permute-start | bytes 98312 | tf_op jit(solution)/shard_map/ppermute | solution.py:21
  54.4 6.7 %collective-permute-start.12 = (bf16[224,512]{1,0:T(8,128)(2,1)S(1)}, bf16[224,512]{1,0:T(8,128)(2,1)S(1)}, u32[]{:S(2)}, u32[]{:S(2)}) collective-permute-start(bf16[224,512]{1,0:T(8,128)(2,1)S(1)} %get-tuple-element.49), channel_id=1, source_target_pairs={{0,30},{2,0},{4,2},{6,4},{8,6},{10,8},{12,10},{14,12},{16,14},{18,... | collective-permute-start | bytes 688136 | tf_op jit(solution)/shard_map/ppermute | solution.py:21
  56.9 8.9 %collective-permute-start.13 = (bf16[224,512]{1,0:T(8,128)(2,1)S(1)}, bf16[224,512]{1,0:T(8,128)(2,1)S(1)}, u32[]{:S(2)}, u32[]{:S(2)}) collective-permute-start(bf16[224,512]{1,0:T(8,128)(2,1)S(1)} %get-tuple-element.48), channel_id=1, source_target_pairs={{0,2},{2,4},{4,6},{6,8},{8,10},{10,12},{12,14},{14,16},{16,18},{18... | collective-permute-start | bytes 688136 | tf_op jit(solution)/shard_map/ppermute | solution.py:21
  56.9 8.9 %collective-permute-start.14 = (bf16[32,512]{1,0:T(8,128)(2,1)S(1)}, bf16[32,512]{1,0:T(8,128)(2,1)S(1)}, u32[]{:S(2)}, u32[]{:S(2)}) collective-permute-start(bf16[32,512]{1,0:T(8,128)(2,1)S(1)} %get-tuple-element.44), channel_id=1, source_target_pairs={{0,4},{2,6},{4,8},{6,10},{8,12},{10,14},{12,16},{14,18},{16,20},{1... | collective-permute-start | bytes 98312 | tf_op jit(solution)/shard_map/ppermute | solution.py:21
  57.0 8.9 %collective-permute-start.15 = (bf16[32,512]{1,0:T(8,128)(2,1)S(1)}, bf16[32,512]{1,0:T(8,128)(2,1)S(1)}, u32[]{:S(2)}, u32[]{:S(2)}) collective-permute-start(bf16[32,512]{1,0:T(8,128)(2,1)S(1)} %get-tuple-element.43), channel_id=1, source_target_pairs={{0,6},{2,8},{4,10},{6,12},{8,14},{10,16},{12,18},{14,20},{16,22},{... | collective-permute-start | bytes 98312 | tf_op jit(solution)/shard_map/ppermute | solution.py:21
  58.7 7.2 %collective-permute-start.16 = (bf16[32,512]{1,0:T(8,128)(2,1)S(1)}, bf16[32,512]{1,0:T(8,128)(2,1)S(1)}, u32[]{:S(2)}, u32[]{:S(2)}) collective-permute-start(bf16[32,512]{1,0:T(8,128)(2,1)S(1)} %get-tuple-element.42), channel_id=1, source_target_pairs={{0,8},{2,10},{4,12},{6,14},{8,16},{10,18},{12,20},{14,22},{16,24},... | collective-permute-start | bytes 98312 | tf_op jit(solution)/shard_map/ppermute | solution.py:21
  61.0 4.9 %collective-permute-start.17 = (bf16[16,512]{1,0:T(8,128)(2,1)S(1)}, bf16[16,512]{1,0:T(8,128)(2,1)S(1)}, u32[]{:S(2)}, u32[]{:S(2)}) collective-permute-start(bf16[16,512]{1,0:T(8,128)(2,1)S(1)} %slice.165), channel_id=1, source_target_pairs={{0,16},{2,18},{4,20},{6,22},{8,24},{10,26},{12,28},{14,30},{16,0},... | collective-permute-start | bytes 49160 | tf_op jit(solution)/shard_map/ppermute | solution.py:21
  65.9 2.8 copy-start.4
  103.3 0.8 copy-start.2
  107.4 15.4 %collective-permute-start.18 = (bf16[32,512]{1,0:T(8,128)(2,1)S(1)}, bf16[32,512]{1,0:T(8,128)(2,1)S(1)}, u32[]{:S(2)}, u32[]{:S(2)}) collective-permute-start(bf16[32,512]{1,0:T(8,128)(2,1)S(1)} %get-tuple-element.39), channel_id=1, source_target_pairs={{0,8},{2,10},{4,12},{6,14},{8,16},{10,18},{12,20},{14,22},{16,24},... | collective-permute-start | bytes 98312 | tf_op jit(solution)/shard_map/ppermute | solution.py:21
  108.4 53.1 %all-to-all-start.1 = ((f32[32,40,128]{2,1,0:T(8,128)}), f32[32,40,128]{2,1,0:T(8,128)S(1)}, u32[]{:S(2)}, u32[]{:S(2)}) async-start(f32[32,40,128]{2,1,0:T(8,128)} %bitcast.21), calls=%async_computation.1 | async-start | bytes 1310720 | tf_op jit(solution)/shard_map/all_to_all | solution.py:482
  115.3 15.5 %collective-permute-start.19 = (bf16[32,512]{1,0:T(8,128)(2,1)S(1)}, bf16[32,512]{1,0:T(8,128)(2,1)S(1)}, u32[]{:S(2)}, u32[]{:S(2)}) collective-permute-start(bf16[32,512]{1,0:T(8,128)(2,1)S(1)} %get-tuple-element.38), channel_id=1, source_target_pairs={{0,6},{2,8},{4,10},{6,12},{8,14},{10,16},{12,18},{14,20},{16,22},{... | collective-permute-start | bytes 98312 | tf_op jit(solution)/shard_map/ppermute | solution.py:21
  116.9 16.5 %collective-permute-start.20 = (bf16[32,512]{1,0:T(8,128)(2,1)S(1)}, bf16[32,512]{1,0:T(8,128)(2,1)S(1)}, u32[]{:S(2)}, u32[]{:S(2)}) collective-permute-start(bf16[32,512]{1,0:T(8,128)(2,1)S(1)} %get-tuple-element.37), channel_id=1, source_target_pairs={{0,4},{2,6},{4,8},{6,10},{8,12},{10,14},{12,16},{14,18},{16,20},{1... | collective-permute-start | bytes 98312 | tf_op jit(solution)/shard_map/ppermute | solution.py:21
  118.4 19.4 %collective-permute-start.21 = (bf16[224,512]{1,0:T(8,128)(2,1)S(1)}, bf16[224,512]{1,0:T(8,128)(2,1)S(1)}, u32[]{:S(2)}, u32[]{:S(2)}) collective-permute-start(bf16[224,512]{1,0:T(8,128)(2,1)S(1)} %get-tuple-element.41), channel_id=1, source_target_pairs={{0,2},{2,4},{4,6},{6,8},{8,10},{10,12},{12,14},{14,16},{16,18},{18... | collective-permute-start | bytes 688136 | tf_op jit(solution)/shard_map/ppermute | solution.py:21
  118.4 21.8 %collective-permute-start.22 = (bf16[224,512]{1,0:T(8,128)(2,1)S(1)}, bf16[224,512]{1,0:T(8,128)(2,1)S(1)}, u32[]{:S(2)}, u32[]{:S(2)}) collective-permute-start(bf16[224,512]{1,0:T(8,128)(2,1)S(1)} %get-tuple-element.40), channel_id=1, source_target_pairs={{0,30},{2,0},{4,2},{6,4},{8,6},{10,8},{12,10},{14,12},{16,14},{18,... | collective-permute-start | bytes 688136 | tf_op jit(solution)/shard_map/ppermute | solution.py:21
  122.8 18.1 %collective-permute-start.23 = (bf16[32,512]{1,0:T(8,128)(2,1)S(1)}, bf16[32,512]{1,0:T(8,128)(2,1)S(1)}, u32[]{:S(2)}, u32[]{:S(2)}) collective-permute-start(bf16[32,512]{1,0:T(8,128)(2,1)S(1)} %get-tuple-element.36), channel_id=1, source_target_pairs={{0,28},{2,30},{4,0},{6,2},{8,4},{10,6},{12,8},{14,10},{16,12},{18,... | collective-permute-start | bytes 98312 | tf_op jit(solution)/shard_map/ppermute | solution.py:21
  130.8 10.7 %collective-permute-start.24 = (bf16[32,512]{1,0:T(8,128)(2,1)S(1)}, bf16[32,512]{1,0:T(8,128)(2,1)S(1)}, u32[]{:S(2)}, u32[]{:S(2)}) collective-permute-start(bf16[32,512]{1,0:T(8,128)(2,1)S(1)} %get-tuple-element.35), channel_id=1, source_target_pairs={{0,26},{2,28},{4,30},{6,0},{8,2},{10,4},{12,6},{14,8},{16,10},{18,... | collective-permute-start | bytes 98312 | tf_op jit(solution)/shard_map/ppermute | solution.py:21
  133.4 8.8 %collective-permute-start.25 = (bf16[32,512]{1,0:T(8,128)(2,1)S(1)}, bf16[32,512]{1,0:T(8,128)(2,1)S(1)}, u32[]{:S(2)}, u32[]{:S(2)}) collective-permute-start(bf16[32,512]{1,0:T(8,128)(2,1)S(1)} %get-tuple-element.34), channel_id=1, source_target_pairs={{0,24},{2,26},{4,28},{6,30},{8,0},{10,2},{12,4},{14,6},{16,8},{18,... | collective-permute-start | bytes 98312 | tf_op jit(solution)/shard_map/ppermute | solution.py:21
  137.8 5.0 %collective-permute-start.26 = (bf16[16,512]{1,0:T(8,128)(2,1)S(1)}, bf16[16,512]{1,0:T(8,128)(2,1)S(1)}, u32[]{:S(2)}, u32[]{:S(2)}) collective-permute-start(bf16[16,512]{1,0:T(8,128)(2,1)S(1)} %slice.176), channel_id=1, source_target_pairs={{0,16},{2,18},{4,20},{6,22},{8,24},{10,26},{12,28},{14,30},{16,0},... | collective-permute-start | bytes 49160 | tf_op jit(solution)/shard_map/ppermute | solution.py:21
  161.5 82.3 %all-to-all-start = ((f32[32,40,128]{2,1,0:T(8,128)}), f32[32,40,128]{2,1,0:T(8,128)S(1)}, u32[]{:S(2)}, u32[]{:S(2)}) async-start(f32[32,40,128]{2,1,0:T(8,128)} %bitcast.18), calls=%async_computation | async-start | bytes 1310720 | tf_op jit(solution)/shard_map/all_to_all | solution.py:482

commit v2 on v1

--- a/solution.py
+++ b/solution.py
@@ -474,19 +474,23 @@
     devices = device_count * samples_count
     axes = ("tile", "tm")
 
-    def summed(grad, bias):
-        rows = jnp.concatenate([grad.reshape(-1, channels), bias], axis=0)
-        used = rows.shape[0]
-        chunk = -(-used // (8 * devices)) * 8
-        rows = jnp.pad(rows, ((0, chunk * devices - used), (0, 0)))
-        parts = lax.all_to_all(rows.reshape(devices, chunk, channels), axes, 0, 0)
-        mine = jnp.sum(parts, axis=0) * grad_scale
-        total = lax.all_gather(mine, axes, axis=0, tiled=True)
-        weight = total[: used - 1].reshape(channels, 3, 3, channels).transpose(1, 2, 3, 0)
-        return weight, total[used - 1]
-
-    grad_weight_two, grad_bias_two = summed(grad_two, sum_two)
-    grad_weight_one, grad_bias_one = summed(grad_one, sum_one)
+    rows = jnp.concatenate(
+        [grad_one.reshape(-1, channels), sum_one, grad_two.reshape(-1, channels), sum_two], axis=0
+    )
+    used = rows.shape[0]
+    chunk = -(-used // (8 * devices)) * 8
+    rows = jnp.pad(rows, ((0, chunk * devices - used), (0, 0)))
+    parts = lax.all_to_all(rows.reshape(devices, chunk, channels), axes, 0, 0)
+    mine = jnp.sum(parts, axis=0) * grad_scale
+    copies = jnp.broadcast_to(mine[None], (devices, chunk, channels))
+    total = lax.all_to_all(copies, axes, 0, 0).reshape(devices * chunk, channels)
+
+    def unpacked(part):
+        weight = part[:-1].reshape(channels, 3, 3, channels).transpose(1, 2, 3, 0)
+        return weight, part[-1]
+
+    grad_weight_one, grad_bias_one = unpacked(total[: used // 2])
+    grad_weight_two, grad_bias_two = unpacked(total[used // 2 : used])
     return (output, grad_weight_one, grad_bias_one, grad_weight_two, grad_bias_two)
 
 

time: 317 us -> 223 us (0.70)
  blocking collectives: 146 us -> 72.1 us
  starting transfers between devices: 50.2 us -> 37.6 us
  waiting for transfers between devices: 12.9 us -> 4.17 us
  local copies, waits for them, and re-layouts: 27.8 us -> 31.3 us
    all_gather x2 -> x0, blocking collectives: 146 us -> none  [summed(): total = lax.all_gather(mine, axes, axis=0, tiled=True)]
    all_to_all x0 -> x2, blocking collectives: none -> 72.1 us  [the longest x1 36.9 us: body(): parts = lax.all_to_all(rows.reshape(devices, chunk, channels), axes, 0, 0)]
    all_to_all x2 -> x0, starting transfers between devices: 10.6 us -> none  [summed(): parts = lax.all_to_all(rows.reshape(devices, chunk, channels), axes, 0, 0)]
    ppermute x27, waiting for transfers between devices: 12.9 us -> 4.17 us  [passed_along(): return lax.ppermute(value, axis, pairs)]
    unnamed x41 -> x39, local copies, waits for them, and re-layouts: 16.3 us -> 18.7 us
  transfers between devices with their start and end apart: 29 -> 27, of which waited for: 4 -> 2; matrix products, arithmetic and copies ran while one was open for 7% -> 8% of each run, Pallas kernels for 4% -> 0%
where the time goes in v2:
time: 223 us; the launch traced here: 222 us
  blocking collectives  72.1 us (32%)
  Pallas kernels  62.1 us (28%)
  starting transfers between devices  37.6 us (17%)
  local copies, waits for them, and re-layouts  31.3 us (14%)
  matrix products  13.2 us (6%)
  waiting for transfers between devices  4.17 us (2%)
    ppermute x27, starting transfers between devices, passed_along(): return lax.ppermute(value, axis, pairs)  37.6 us
    all_to_all x1, blocking collectives, body(): parts = lax.all_to_all(rows.reshape(devices, chunk, channels), axes, 0, 0)  36.9 us
    all_to_all x1, blocking collectives, body(): lax.all_to_all(copies, axes, 0, 0).reshape(devices * chunk, channels)  35.3 us
    pallas_call x1, Pallas kernels, body(): pl.pallas_call(second_kernel, grid=(per_device,), in_specs=[per_tile(tile...  34.6 us
    unnamed x39, local copies, waits for them, and re-layouts  18.7 us
    pallas_call x1, Pallas kernels, body(): pl.pallas_call(first_kernel, grid=(per_device,), in_specs=[per_tile(tile_...  14 us
    pallas_call x1, Pallas kernels, body(): pl.pallas_call(third_kernel, grid=(per_device,), in_specs=[per_tile(tile_...  13.5 us
    dot_general x2, matrix products, halo_of(): return jnp.dot(one_hot(receive, tile_index, pool.shape[0]), pool)  6.96 us
  transfers between devices with their start and end apart: 27, of which 2 were waited for; matrix products, arithmetic and copies ran while one was open for 8% of the time, Pallas kernels for 0%

profile of v2, /device:TPU:0, one launch (start us, length us, event | category | flops | bytes accessed | tf_op | source)
XLA Modules:
  0.0 221.7 jit_solution(15923303325838168002)
XLA Ops:
  0.6 2.7 %fusion.14 = (bf16[12,4,16,1,128]{4,3,2,1,0:T(2,128)(2,1)S(1)}, bf16[12,4,16,1,128]{4,3,2,1,0:T(2,128)(2,1)S(1)}) fusion(bf16[12,4,16,16,128]{4,3,2,1,0:T(8,128)(2,1)} %x_ref.3), kind=kLoop, calls=%fused_computation.61 | loop fusion | bytes 786432 | tf_op jit(solution)/shard_map/slice | solution.py:423
  3.3 1.1 slice_bitcast_fusion.1
  5.2 0.8 dynamic-slice_reduce_fusion.2
  6.0 0.7 fusion.8
  6.8 5.1 %collective-permute-start = (bf16[32,512]{1,0:T(8,128)(2,1)S(1)}, bf16[32,512]{1,0:T(8,128)(2,1)S(1)}, u32[]{:S(2)}, u32[]{:S(2)}) collective-permute-start(bf16[32,512]{1,0:T(8,128)(2,1)S(1)} %get-tuple-element.59), channel_id=1, source_target_pairs={{0,24},{2,26},{4,28},{6,30},{8,0},{10,2},{12,4},{14,6},{16,8},{18,... | collective-permute-start | bytes 98312 | tf_op jit(solution)/shard_map/ppermute | solution.py:21
  11.9 1.4 collective-permute-start.2
  13.3 1.4 collective-permute-start.3
  14.7 1.0 bitcast_dynamic-update-slice_fusion
  16.2 0.8 dynamic-slice_reduce_fusion.1
  17.0 0.9 dynamic-slice_reduce_fusion
  19.2 2.5 %collective-permute-start.6 = (bf16[32,512]{1,0:T(8,128)(2,1)S(1)}, bf16[32,512]{1,0:T(8,128)(2,1)S(1)}, u32[]{:S(2)}, u32[]{:S(2)}) collective-permute-start(bf16[32,512]{1,0:T(8,128)(2,1)S(1)} %get-tuple-element.55), channel_id=1, source_target_pairs={{0,6},{2,8},{4,10},{6,12},{8,14},{10,16},{12,18},{14,20},{16,22},{... | collective-permute-start | bytes 98312 | tf_op jit(solution)/shard_map/ppermute | solution.py:21
  22.3 1.2 collective-permute-start.7
  24.2 1.6 collective-permute-start.8
  25.8 0.7 constant_dynamic-update-slice_fusion.5
  26.5 0.7 constant_dynamic-update-slice_fusion.4
  29.7 4.2 %fusion.1 = bf16[1536,512]{1,0:T(8,128)(2,1)S(1)} fusion(bf16[1424,512]{1,0:T(8,128)(2,1)} %constant_dynamic-update-slice_fusion, s32[1536]{0:T(1024)S(1)} %dynamic-slice_reduce_fusion.1), kind=kOutput, calls=%fused_computation.2 | convolution fusion | flops 2241945600 | bytes 3037184 | tf_op jit(solution)/shard_map/dot_general | solution.py:222
  33.9 14.0 %shard_map.155 = (bf16[12,4,16,16,128]{4,3,2,1,0:T(8,128)(2,1)S(1)}, f32[12,4,256,128]{3,2,1,0:T(8,128)}, bf16[12,64,512]{2,1,0:T(8,128)(2,1)S(1)}) custom-call(bf16[12,4,16,16,128]{4,3,2,1,0:T(8,128)(2,1)} %x_ref.3, bf16[12,128,512]{2,1,0:T(8,128)(2,1)S(1)} %bitcast.46, bf16[1152,128]{1,0:T(8,128)(2,1)S(1)} %bitcast.58, f32[1,128]{1,0:T(1,128)S(1)} %bitcast.60), custom_call_target="tpu_custom_call" | custom-call | tf_op jit(solution)/shard_map/pallas_call | solution.py:427
  47.8 0.7 fusion.7
  48.6 0.9 copy-done
  49.5 2.5 %collective-permute-start.9 = (bf16[32,512]{1,0:T(8,128)(2,1)S(1)}, bf16[32,512]{1,0:T(8,128)(2,1)S(1)}, u32[]{:S(2)}, u32[]{:S(2)}) collective-permute-start(bf16[32,512]{1,0:T(8,128)(2,1)S(1)} %get-tuple-element.51), channel_id=1, source_target_pairs={{0,24},{2,26},{4,28},{6,30},{8,0},{10,2},{12,4},{14,6},{16,8},{18,... | collective-permute-start | bytes 98312 | tf_op jit(solution)/shard_map/ppermute | solution.py:21
  52.1 2.3 %collective-permute-start.11 = (bf16[32,512]{1,0:T(8,128)(2,1)S(1)}, bf16[32,512]{1,0:T(8,128)(2,1)S(1)}, u32[]{:S(2)}, u32[]{:S(2)}) collective-permute-start(bf16[32,512]{1,0:T(8,128)(2,1)S(1)} %get-tuple-element.49), channel_id=1, source_target_pairs={{0,28},{2,30},{4,0},{6,2},{8,4},{10,6},{12,8},{14,10},{16,12},{18,... | collective-permute-start | bytes 98312 | tf_op jit(solution)/shard_map/ppermute | solution.py:21
  54.4 2.5 %collective-permute-start.12 = (bf16[224,512]{1,0:T(8,128)(2,1)S(1)}, bf16[224,512]{1,0:T(8,128)(2,1)S(1)}, u32[]{:S(2)}, u32[]{:S(2)}) collective-permute-start(bf16[224,512]{1,0:T(8,128)(2,1)S(1)} %get-tuple-element.53), channel_id=1, source_target_pairs={{0,30},{2,0},{4,2},{6,4},{8,6},{10,8},{12,10},{14,12},{16,14},{18,... | collective-permute-start | bytes 688136 | tf_op jit(solution)/shard_map/ppermute | solution.py:21
  57.0 1.7 collective-permute-start.15
  58.7 1.5 collective-permute-start.16
  60.2 0.9 collective-permute-done.12
  61.0 1.6 collective-permute-start.17
  62.6 3.2 %collective-permute-done.13 = bf16[224,512]{1,0:T(8,128)(2,1)S(1)} collective-permute-done((bf16[224,512]{1,0:T(8,128)(2,1)S(1)}, bf16[224,512]{1,0:T(8,128)(2,1)S(1)}, u32[]{:S(2)}, u32[]{:S(2)}) %collective-permute-start.13) | collective-permute-done | bytes 229408 | tf_op jit(solution)/shard_map/ppermute | solution.py:21
  66.0 2.8 %fusion = bf16[1536,512]{1,0:T(8,128)(2,1)S(1)} fusion(bf16[1424,512]{1,0:T(8,128)(2,1)S(1)} %constant_dynamic-update-slice_fusion.9, s32[1536]{0:T(1024)S(1)} %dynamic-slice_reduce_fusion.1), kind=kOutput, calls=%fused_computation.1 | convolution fusion | flops 2241945600 | bytes 3037184 | tf_op jit(solution)/shard_map/dot_general | solution.py:222
  68.8 34.6 %shard_map.156 = (bf16[12,4,16,16,128]{4,3,2,1,0:T(8,128)(2,1)}, f32[12,4,256,128]{3,2,1,0:T(8,128)}, bf16[12,96,512]{2,1,0:T(8,128)(2,1)S(1)}, f32[128,1152]{1,0:T(8,128)S(1)}, f32[1,128]{1,0:T(1,128)S(1)}) custom-call(bf16[12,4,16,16,128]{4,3,2,1,0:T(8,128)(2,1)} %copy-done, bf16[12,128,512]{2,1,0:T(8,128)(2,1)S(1)} %bitcast.52, ...), custom_call_target="tpu_custom_call" | custom-call | tf_op jit(solution)/shard_map/pallas_call | solution.py:437
  103.3 1.1 constant_dynamic-update-slice_fusion.28
  104.4 1.1 fusion.5
  106.8 2.0 collective-permute-start.19
  108.8 2.0 collective-permute-start.20
  110.7 4.4 %collective-permute-start.22 = (bf16[224,512]{1,0:T(8,128)(2,1)S(1)}, bf16[224,512]{1,0:T(8,128)(2,1)S(1)}, u32[]{:S(2)}, u32[]{:S(2)}) collective-permute-start(bf16[224,512]{1,0:T(8,128)(2,1)S(1)} %get-tuple-element.44), channel_id=1, source_target_pairs={{0,30},{2,0},{4,2},{6,4},{8,6},{10,8},{12,10},{14,12},{16,14},{18,... | collective-permute-start | bytes 688136 | tf_op jit(solution)/shard_map/ppermute | solution.py:21
  115.6 1.4 constant_dynamic-update-slice_fusion.27
  117.0 1.2 collective-permute-start.24
  118.1 1.4 constant_dynamic-update-slice_fusion.26
  119.8 1.4 constant_dynamic-update-slice_fusion.25
  121.2 1.4 collective-permute-start.26
  122.6 1.6 constant_dynamic-update-slice_fusion.24
  124.2 0.7 constant_dynamic-update-slice_fusion.23
  127.4 3.7 %fusion.2 = f32[768,512]{1,0:T(8,128)S(1)} fusion(bf16[1808,512]{1,0:T(8,128)(2,1)} %constant_dynamic-update-slice_fusion.19, s32[1808]{0:T(1024)S(1)} %dynamic-slice_reduce_fusion), kind=kOutput, calls=%fused_computation.4 | convolution fusion | flops 1423257600 | bytes 3431488 | tf_op jit(solution)/shard_map/dot_general | solution.py:230
  131.1 13.5 %shard_map.157 = (f32[128,1152]{1,0:T(8,128)S(1)}, f32[1,128]{1,0:T(1,128)S(1)}) custom-call(bf16[12,4,16,16,128]{4,3,2,1,0:T(8,128)(2,1)} %x_ref.3, bf16[12,128,512]{2,1,0:T(8,128)(2,1)S(1)} %bitcast.47, f32[12,4,256,128]{3,2,1,0:T(8,128)} %get-tuple-element.18.inner_ref, f32[12,64,512]{2,1,0:T(8,128)S(1)} %bitcast.51, ...), custom_call_target="tpu_custom_call" | custom-call | tf_op jit(solution)/shard_map/pallas_call | solution.py:459
  144.7 1.2 concatenate.20
  146.0 36.9 %all_to_all.10 = f32[32,80,128]{2,1,0:T(8,128)S(1)} all-to-all(f32[32,80,128]{2,1,0:T(8,128)S(1)} %bitcast.61), channel_id=1, replica_groups=mesh['tile'=16,'tm'=2] {'tile','tm'}, dimensions={0} | all-to-all | bytes 2621440 | tf_op jit(solution)/shard_map/all_to_all | solution.py:483
  183.0 35.3 %all_to_all.11 = f32[32,80,128]{2,1,0:T(8,128)S(1)} all-to-all(f32[32,80,128]{2,1,0:T(8,128)S(1)} %broadcast_in_dim.2), channel_id=1, replica_groups=mesh['tile'=16,'tm'=2] {'tile','tm'}, dimensions={0} | all-to-all | bytes 2621440 | tf_op jit(solution)/shard_map/all_to_all | solution.py:486
  219.2 1.1 copy.31
  220.5 1.1 copy.32
  (92 shorter events, 12.5 us)
Async XLA Ops:
  6.7 9.0 %copy-start.1 = (bf16[3,3,128,128]{3,2,1,0:T(8,128)(2,1)S(1)}, bf16[3,3,128,128]{3,2,1,0:T(8,128)(2,1)}, u32[]{:S(2)}) copy-start(bf16[3,3,128,128]{3,2,1,0:T(8,128)(2,1)} %param.15) | copy-start | bytes 884740
  6.8 11.2 %collective-permute-start = (bf16[32,512]{1,0:T(8,128)(2,1)S(1)}, bf16[32,512]{1,0:T(8,128)(2,1)S(1)}, u32[]{:S(2)}, u32[]{:S(2)}) collective-permute-start(bf16[32,512]{1,0:T(8,128)(2,1)S(1)} %get-tuple-element.59), channel_id=1, source_target_pairs={{0,24},{2,26},{4,28},{6,30},{8,0},{10,2},{12,4},{14,6},{16,8},{18,... | collective-permute-start | bytes 98312 | tf_op jit(solution)/shard_map/ppermute | solution.py:21
  11.9 7.4 %collective-permute-start.1 = (bf16[32,512]{1,0:T(8,128)(2,1)S(1)}, bf16[32,512]{1,0:T(8,128)(2,1)S(1)}, u32[]{:S(2)}, u32[]{:S(2)}) collective-permute-start(bf16[32,512]{1,0:T(8,128)(2,1)S(1)} %get-tuple-element.58), channel_id=1, source_target_pairs={{0,26},{2,28},{4,30},{6,0},{8,2},{10,4},{12,6},{14,8},{16,10},{18,... | collective-permute-start | bytes 98312 | tf_op jit(solution)/shard_map/ppermute | solution.py:21
  11.9 10.5 %collective-permute-start.2 = (bf16[32,512]{1,0:T(8,128)(2,1)S(1)}, bf16[32,512]{1,0:T(8,128)(2,1)S(1)}, u32[]{:S(2)}, u32[]{:S(2)}) collective-permute-start(bf16[32,512]{1,0:T(8,128)(2,1)S(1)} %get-tuple-element.57), channel_id=1, source_target_pairs={{0,28},{2,30},{4,0},{6,2},{8,4},{10,6},{12,8},{14,10},{16,12},{18,... | collective-permute-start | bytes 98312 | tf_op jit(solution)/shard_map/ppermute | solution.py:21
  13.3 10.9 %collective-permute-start.3 = (bf16[224,512]{1,0:T(8,128)(2,1)S(1)}, bf16[224,512]{1,0:T(8,128)(2,1)S(1)}, u32[]{:S(2)}, u32[]{:S(2)}) collective-permute-start(bf16[224,512]{1,0:T(8,128)(2,1)S(1)} %get-tuple-element.61), channel_id=1, source_target_pairs={{0,30},{2,0},{4,2},{6,4},{8,6},{10,8},{12,10},{14,12},{16,14},{18,... | collective-permute-start | bytes 688136 | tf_op jit(solution)/shard_map/ppermute | solution.py:21
  14.7 11.8 %collective-permute-start.4 = (bf16[224,512]{1,0:T(8,128)(2,1)S(1)}, bf16[224,512]{1,0:T(8,128)(2,1)S(1)}, u32[]{:S(2)}, u32[]{:S(2)}) collective-permute-start(bf16[224,512]{1,0:T(8,128)(2,1)S(1)} %get-tuple-element.60), channel_id=1, source_target_pairs={{0,2},{2,4},{4,6},{6,8},{8,10},{10,12},{12,14},{14,16},{16,18},{18... | collective-permute-start | bytes 688136 | tf_op jit(solution)/shard_map/ppermute | solution.py:21
  17.9 9.3 %collective-permute-start.5 = (bf16[32,512]{1,0:T(8,128)(2,1)S(1)}, bf16[32,512]{1,0:T(8,128)(2,1)S(1)}, u32[]{:S(2)}, u32[]{:S(2)}) collective-permute-start(bf16[32,512]{1,0:T(8,128)(2,1)S(1)} %get-tuple-element.56), channel_id=1, source_target_pairs={{0,4},{2,6},{4,8},{6,10},{8,12},{10,14},{12,16},{14,18},{16,20},{1... | collective-permute-start | bytes 98312 | tf_op jit(solution)/shard_map/ppermute | solution.py:21
  19.2 8.6 %collective-permute-start.6 = (bf16[32,512]{1,0:T(8,128)(2,1)S(1)}, bf16[32,512]{1,0:T(8,128)(2,1)S(1)}, u32[]{:S(2)}, u32[]{:S(2)}) collective-permute-start(bf16[32,512]{1,0:T(8,128)(2,1)S(1)} %get-tuple-element.55), channel_id=1, source_target_pairs={{0,6},{2,8},{4,10},{6,12},{8,14},{10,16},{12,18},{14,20},{16,22},{... | collective-permute-start | bytes 98312 | tf_op jit(solution)/shard_map/ppermute | solution.py:21
  22.3 6.1 %collective-permute-start.7 = (bf16[32,512]{1,0:T(8,128)(2,1)S(1)}, bf16[32,512]{1,0:T(8,128)(2,1)S(1)}, u32[]{:S(2)}, u32[]{:S(2)}) collective-permute-start(bf16[32,512]{1,0:T(8,128)(2,1)S(1)} %get-tuple-element.54), channel_id=1, source_target_pairs={{0,8},{2,10},{4,12},{6,14},{8,16},{10,18},{12,20},{14,22},{16,24},... | collective-permute-start | bytes 98312 | tf_op jit(solution)/shard_map/ppermute | solution.py:21
  24.2 4.9 %collective-permute-start.8 = (bf16[16,512]{1,0:T(8,128)(2,1)S(1)}, bf16[16,512]{1,0:T(8,128)(2,1)S(1)}, u32[]{:S(2)}, u32[]{:S(2)}) collective-permute-start(bf16[16,512]{1,0:T(8,128)(2,1)S(1)} %slice.162), channel_id=1, source_target_pairs={{0,16},{2,18},{4,20},{6,22},{8,24},{10,26},{12,28},{14,30},{16,0},... | collective-permute-start | bytes 49160 | tf_op jit(solution)/shard_map/ppermute | solution.py:21
  29.7 4.2 %copy-start.2 = (bf16[3,3,128,128]{3,2,1,0:T(8,128)(2,1)S(1)}, bf16[3,3,128,128]{3,2,1,0:T(8,128)(2,1)}, u32[]{:S(2)}) copy-start(bf16[3,3,128,128]{3,2,1,0:T(8,128)(2,1)} %param.13) | copy-start | bytes 884740
  29.7 4.2 %copy-start.4 = (f32[128]{0:T(128)S(1)}, f32[128]{0:T(128)}, u32[]{:S(2)}) copy-start(f32[128]{0:T(128)} %param.14) | copy-start | bytes 1540
  47.8 1.6 copy-start
  49.5 7.4 %collective-permute-start.9 = (bf16[32,512]{1,0:T(8,128)(2,1)S(1)}, bf16[32,512]{1,0:T(8,128)(2,1)S(1)}, u32[]{:S(2)}, u32[]{:S(2)}) collective-permute-start(bf16[32,512]{1,0:T(8,128)(2,1)S(1)} %get-tuple-element.51), channel_id=1, source_target_pairs={{0,24},{2,26},{4,28},{6,30},{8,0},{10,2},{12,4},{14,6},{16,8},{18,... | collective-permute-start | bytes 98312 | tf_op jit(solution)/shard_map/ppermute | solution.py:21
  52.1 4.9 %collective-permute-start.10 = (bf16[32,512]{1,0:T(8,128)(2,1)S(1)}, bf16[32,512]{1,0:T(8,128)(2,1)S(1)}, u32[]{:S(2)}, u32[]{:S(2)}) collective-permute-start(bf16[32,512]{1,0:T(8,128)(2,1)S(1)} %get-tuple-element.50), channel_id=1, source_target_pairs={{0,26},{2,28},{4,30},{6,0},{8,2},{10,4},{12,6},{14,8},{16,10},{18,... | collective-permute-start | bytes 98312 | tf_op jit(solution)/shard_map/ppermute | solution.py:21
  52.1 6.5 %collective-permute-start.11 = (bf16[32,512]{1,0:T(8,128)(2,1)S(1)}, bf16[32,512]{1,0:T(8,128)(2,1)S(1)}, u32[]{:S(2)}, u32[]{:S(2)}) collective-permute-start(bf16[32,512]{1,0:T(8,128)(2,1)S(1)} %get-tuple-element.49), channel_id=1, source_target_pairs={{0,28},{2,30},{4,0},{6,2},{8,4},{10,6},{12,8},{14,10},{16,12},{18,... | collective-permute-start | bytes 98312 | tf_op jit(solution)/shard_map/ppermute | solution.py:21
  54.4 6.7 %collective-permute-start.12 = (bf16[224,512]{1,0:T(8,128)(2,1)S(1)}, bf16[224,512]{1,0:T(8,128)(2,1)S(1)}, u32[]{:S(2)}, u32[]{:S(2)}) collective-permute-start(bf16[224,512]{1,0:T(8,128)(2,1)S(1)} %get-tuple-element.53), channel_id=1, source_target_pairs={{0,30},{2,0},{4,2},{6,4},{8,6},{10,8},{12,10},{14,12},{16,14},{18,... | collective-permute-start | bytes 688136 | tf_op jit(solution)/shard_map/ppermute | solution.py:21
  56.9 8.9 %collective-permute-start.13 = (bf16[224,512]{1,0:T(8,128)(2,1)S(1)}, bf16[224,512]{1,0:T(8,128)(2,1)S(1)}, u32[]{:S(2)}, u32[]{:S(2)}) collective-permute-start(bf16[224,512]{1,0:T(8,128)(2,1)S(1)} %get-tuple-element.52), channel_id=1, source_target_pairs={{0,2},{2,4},{4,6},{6,8},{8,10},{10,12},{12,14},{14,16},{16,18},{18... | collective-permute-start | bytes 688136 | tf_op jit(solution)/shard_map/ppermute | solution.py:21
  56.9 8.9 %collective-permute-start.14 = (bf16[32,512]{1,0:T(8,128)(2,1)S(1)}, bf16[32,512]{1,0:T(8,128)(2,1)S(1)}, u32[]{:S(2)}, u32[]{:S(2)}) collective-permute-start(bf16[32,512]{1,0:T(8,128)(2,1)S(1)} %get-tuple-element.48), channel_id=1, source_target_pairs={{0,4},{2,6},{4,8},{6,10},{8,12},{10,14},{12,16},{14,18},{16,20},{1... | collective-permute-start | bytes 98312 | tf_op jit(solution)/shard_map/ppermute | solution.py:21
  57.0 8.9 %collective-permute-start.15 = (bf16[32,512]{1,0:T(8,128)(2,1)S(1)}, bf16[32,512]{1,0:T(8,128)(2,1)S(1)}, u32[]{:S(2)}, u32[]{:S(2)}) collective-permute-start(bf16[32,512]{1,0:T(8,128)(2,1)S(1)} %get-tuple-element.47), channel_id=1, source_target_pairs={{0,6},{2,8},{4,10},{6,12},{8,14},{10,16},{12,18},{14,20},{16,22},{... | collective-permute-start | bytes 98312 | tf_op jit(solution)/shard_map/ppermute | solution.py:21
  58.7 7.2 %collective-permute-start.16 = (bf16[32,512]{1,0:T(8,128)(2,1)S(1)}, bf16[32,512]{1,0:T(8,128)(2,1)S(1)}, u32[]{:S(2)}, u32[]{:S(2)}) collective-permute-start(bf16[32,512]{1,0:T(8,128)(2,1)S(1)} %get-tuple-element.46), channel_id=1, source_target_pairs={{0,8},{2,10},{4,12},{6,14},{8,16},{10,18},{12,20},{14,22},{16,24},... | collective-permute-start | bytes 98312 | tf_op jit(solution)/shard_map/ppermute | solution.py:21
  61.0 4.9 %collective-permute-start.17 = (bf16[16,512]{1,0:T(8,128)(2,1)S(1)}, bf16[16,512]{1,0:T(8,128)(2,1)S(1)}, u32[]{:S(2)}, u32[]{:S(2)}) collective-permute-start(bf16[16,512]{1,0:T(8,128)(2,1)S(1)} %slice.171), channel_id=1, source_target_pairs={{0,16},{2,18},{4,20},{6,22},{8,24},{10,26},{12,28},{14,30},{16,0},... | collective-permute-start | bytes 49160 | tf_op jit(solution)/shard_map/ppermute | solution.py:21
  65.9 2.8 %copy-start.3 = (f32[128]{0:T(128)S(1)}, f32[128]{0:T(128)}, u32[]{:S(2)}) copy-start(f32[128]{0:T(128)} %param.16) | copy-start | bytes 1540
  106.1 9.1 %collective-permute-start.18 = (bf16[32,512]{1,0:T(8,128)(2,1)}, bf16[32,512]{1,0:T(8,128)(2,1)}, u32[]{:S(2)}, u32[]{:S(2)}) collective-permute-start(bf16[32,512]{1,0:T(8,128)(2,1)} %get-tuple-element.43), channel_id=1, source_target_pairs={{0,8},{2,10},{4,12},{6,14},{8,16},{10,18},{12,20},{14,22},{16,24},... | collective-permute-start | bytes 98312 | tf_op jit(solution)/shard_map/ppermute | solution.py:21
  106.8 10.2 %collective-permute-start.19 = (bf16[32,512]{1,0:T(8,128)(2,1)}, bf16[32,512]{1,0:T(8,128)(2,1)}, u32[]{:S(2)}, u32[]{:S(2)}) collective-permute-start(bf16[32,512]{1,0:T(8,128)(2,1)} %get-tuple-element.42), channel_id=1, source_target_pairs={{0,6},{2,8},{4,10},{6,12},{8,14},{10,16},{12,18},{14,20},{16,22},{... | collective-permute-start | bytes 98312 | tf_op jit(solution)/shard_map/ppermute | solution.py:21
  108.8 10.7 %collective-permute-start.20 = (bf16[32,512]{1,0:T(8,128)(2,1)}, bf16[32,512]{1,0:T(8,128)(2,1)}, u32[]{:S(2)}, u32[]{:S(2)}) collective-permute-start(bf16[32,512]{1,0:T(8,128)(2,1)} %get-tuple-element.41), channel_id=1, source_target_pairs={{0,4},{2,6},{4,8},{6,10},{8,12},{10,14},{12,16},{14,18},{16,20},{1... | collective-permute-start | bytes 98312 | tf_op jit(solution)/shard_map/ppermute | solution.py:21
  110.7 10.5 %collective-permute-start.21 = (bf16[224,512]{1,0:T(8,128)(2,1)S(1)}, bf16[224,512]{1,0:T(8,128)(2,1)}, u32[]{:S(2)}, u32[]{:S(2)}) collective-permute-start(bf16[224,512]{1,0:T(8,128)(2,1)S(1)} %get-tuple-element.45), channel_id=1, source_target_pairs={{0,2},{2,4},{4,6},{6,8},{8,10},{10,12},{12,14},{14,16},{16,18},{18... | collective-permute-start | bytes 688136 | tf_op jit(solution)/shard_map/ppermute | solution.py:21
  110.7 13.5 %collective-permute-start.22 = (bf16[224,512]{1,0:T(8,128)(2,1)S(1)}, bf16[224,512]{1,0:T(8,128)(2,1)S(1)}, u32[]{:S(2)}, u32[]{:S(2)}) collective-permute-start(bf16[224,512]{1,0:T(8,128)(2,1)S(1)} %get-tuple-element.44), channel_id=1, source_target_pairs={{0,30},{2,0},{4,2},{6,4},{8,6},{10,8},{12,10},{14,12},{16,14},{18,... | collective-permute-start | bytes 688136 | tf_op jit(solution)/shard_map/ppermute | solution.py:21
  115.2 9.7 %collective-permute-start.23 = (bf16[32,512]{1,0:T(8,128)(2,1)S(1)}, bf16[32,512]{1,0:T(8,128)(2,1)S(1)}, u32[]{:S(2)}, u32[]{:S(2)}) collective-permute-start(bf16[32,512]{1,0:T(8,128)(2,1)S(1)} %get-tuple-element.40), channel_id=1, source_target_pairs={{0,28},{2,30},{4,0},{6,2},{8,4},{10,6},{12,8},{14,10},{16,12},{18,... | collective-permute-start | bytes 98312 | tf_op jit(solution)/shard_map/ppermute | solution.py:21
  117.0 8.6 %collective-permute-start.24 = (bf16[32,512]{1,0:T(8,128)(2,1)S(1)}, bf16[32,512]{1,0:T(8,128)(2,1)S(1)}, u32[]{:S(2)}, u32[]{:S(2)}) collective-permute-start(bf16[32,512]{1,0:T(8,128)(2,1)S(1)} %get-tuple-element.39), channel_id=1, source_target_pairs={{0,26},{2,28},{4,30},{6,0},{8,2},{10,4},{12,6},{14,8},{16,10},{18,... | collective-permute-start | bytes 98312 | tf_op jit(solution)/shard_map/ppermute | solution.py:21
  119.5 6.7 %collective-permute-start.25 = (bf16[32,512]{1,0:T(8,128)(2,1)S(1)}, bf16[32,512]{1,0:T(8,128)(2,1)S(1)}, u32[]{:S(2)}, u32[]{:S(2)}) collective-permute-start(bf16[32,512]{1,0:T(8,128)(2,1)S(1)} %get-tuple-element.38), channel_id=1, source_target_pairs={{0,24},{2,26},{4,28},{6,30},{8,0},{10,2},{12,4},{14,6},{16,8},{18,... | collective-permute-start | bytes 98312 | tf_op jit(solution)/shard_map/ppermute | solution.py:21
  121.2 5.6 %collective-permute-start.26 = (bf16[16,512]{1,0:T(8,128)(2,1)}, bf16[16,512]{1,0:T(8,128)(2,1)S(1)}, u32[]{:S(2)}, u32[]{:S(2)}) collective-permute-start(bf16[16,512]{1,0:T(8,128)(2,1)} %slice.182), channel_id=1, source_target_pairs={{0,16},{2,18},{4,20},{6,22},{8,24},{10,26},{12,28},{14,30},{16,0},... | collective-permute-start | bytes 49160 | tf_op jit(solution)/shard_map/ppermute | solution.py:21

commit v3 on v1

--- a/solution.py
+++ b/solution.py
@@ -480,8 +480,9 @@
         chunk = -(-used // (8 * devices)) * 8
         rows = jnp.pad(rows, ((0, chunk * devices - used), (0, 0)))
         parts = lax.all_to_all(rows.reshape(devices, chunk, channels), axes, 0, 0)
-        mine = jnp.sum(parts, axis=0) * grad_scale
-        total = lax.all_gather(mine, axes, axis=0, tiled=True)
+        mine = (jnp.sum(parts, axis=0) * grad_scale).astype(bf16)
+        copies = jnp.broadcast_to(mine[None], (devices, chunk, channels))
+        total = lax.all_to_all(copies, axes, 0, 0).reshape(devices * chunk, channels).astype(f32)
         weight = total[: used - 1].reshape(channels, 3, 3, channels).transpose(1, 2, 3, 0)
         return weight, total[used - 1]
 

time: 317 us -> 218 us (0.69)
  blocking collectives: 146 us -> 0 us
  waiting for transfers between devices: 12.9 us -> 52 us
  starting transfers between devices: 50.2 us -> 56.5 us
    all_gather x2 -> x0, blocking collectives: 146 us -> none  [summed(): total = lax.all_gather(mine, axes, axis=0, tiled=True)]
    all_to_all x0 -> x2, waiting for transfers between devices: none -> 21.4 us  [summed(): lax.all_to_all(copies, axes, 0, 0).reshape(devices * chunk, channels)]
    all_to_all x2, waiting for transfers between devices: 0.01 us -> 17.7 us  [summed(): parts = lax.all_to_all(rows.reshape(devices, chunk, channels), axes, 0, 0)]
    all_to_all x0 -> x2, starting transfers between devices: none -> 6.31 us  [summed(): lax.all_to_all(copies, axes, 0, 0).reshape(devices * chunk, channels)]
  transfers between devices with their start and end apart: 29 -> 31, of which waited for: 4 -> 7; matrix products, arithmetic and copies ran while one was open for 7% -> 10% of each run, Pallas kernels for 4% -> 6%
where the time goes in v3:
time: 218 us; the launch traced here: 216 us
  Pallas kernels  62.1 us (28%)
  starting transfers between devices  56.5 us (26%)
  waiting for transfers between devices  52 us (24%)
  local copies, waits for them, and re-layouts  29.3 us (13%)
  matrix products  13.2 us (6%)
    ppermute x27, starting transfers between devices, passed_along(): return lax.ppermute(value, axis, pairs)  39.6 us
    pallas_call x1, Pallas kernels, body(): pl.pallas_call(second_kernel, grid=(per_device,), in_specs=[per_tile(tile...  34.6 us
    all_to_all x2, waiting for transfers between devices, summed(): lax.all_to_all(copies, axes, 0, 0).reshape(devices * chunk, channels)  21.4 us
    all_to_all x2, waiting for transfers between devices, summed(): parts = lax.all_to_all(rows.reshape(devices, chunk, channels), axes, 0, 0)  17.7 us
    unnamed x41, local copies, waits for them, and re-layouts  16.3 us
    pallas_call x1, Pallas kernels, body(): pl.pallas_call(first_kernel, grid=(per_device,), in_specs=[per_tile(tile_...  14 us
    pallas_call x1, Pallas kernels, body(): pl.pallas_call(third_kernel, grid=(per_device,), in_specs=[per_tile(tile_...  13.5 us
    ppermute x27, waiting for transfers between devices, passed_along(): return lax.ppermute(value, axis, pairs)  12.9 us
  transfers between devices with their start and end apart: 31, of which 7 were waited for; matrix products, arithmetic and copies ran while one was open for 10% of the time, Pallas kernels for 6%

profile of v3, /device:TPU:0, one launch (start us, length us, event | category | flops | bytes accessed | tf_op | source)
XLA Modules:
  0.0 216.4 jit_solution(4522354504640045378)
XLA Ops:
  0.6 2.7 %fusion.14 = (bf16[12,4,16,1,128]{4,3,2,1,0:T(2,128)(2,1)S(1)}, bf16[12,4,16,1,128]{4,3,2,1,0:T(2,128)(2,1)S(1)}) fusion(bf16[12,4,16,16,128]{4,3,2,1,0:T(8,128)(2,1)} %x_ref.3), kind=kLoop, calls=%fused_computation.67 | loop fusion | bytes 786432 | tf_op jit(solution)/shard_map/slice | solution.py:423
  3.3 1.1 slice_bitcast_fusion.1
  6.8 5.1 %collective-permute-start = (bf16[32,512]{1,0:T(8,128)(2,1)S(1)}, bf16[32,512]{1,0:T(8,128)(2,1)S(1)}, u32[]{:S(2)}, u32[]{:S(2)}) collective-permute-start(bf16[32,512]{1,0:T(8,128)(2,1)S(1)} %get-tuple-element.55), channel_id=1, source_target_pairs={{0,24},{2,26},{4,28},{6,30},{8,0},{10,2},{12,4},{14,6},{16,8},{18,... | collective-permute-start | bytes 98312 | tf_op jit(solution)/shard_map/ppermute | solution.py:21
  11.9 1.4 collective-permute-start.2
  13.3 1.4 collective-permute-start.3
  14.7 1.0 bitcast_dynamic-update-slice_fusion
  16.2 0.8 dynamic-slice_reduce_fusion.1
  17.0 0.9 dynamic-slice_reduce_fusion
  19.2 2.5 %collective-permute-start.6 = (bf16[32,512]{1,0:T(8,128)(2,1)S(1)}, bf16[32,512]{1,0:T(8,128)(2,1)S(1)}, u32[]{:S(2)}, u32[]{:S(2)}) collective-permute-start(bf16[32,512]{1,0:T(8,128)(2,1)S(1)} %get-tuple-element.51), channel_id=1, source_target_pairs={{0,6},{2,8},{4,10},{6,12},{8,14},{10,16},{12,18},{14,20},{16,22},{... | collective-permute-start | bytes 98312 | tf_op jit(solution)/shard_map/ppermute | solution.py:21
  22.3 1.2 collective-permute-start.7
  24.2 1.6 collective-permute-start.8
  29.7 4.2 %fusion.1 = bf16[1536,512]{1,0:T(8,128)(2,1)S(1)} fusion(bf16[1424,512]{1,0:T(8,128)(2,1)} %constant_dynamic-update-slice_fusion, s32[1536]{0:T(1024)S(1)} %dynamic-slice_reduce_fusion.1), kind=kOutput, calls=%fused_computation.2 | convolution fusion | flops 2241945600 | bytes 3037184 | tf_op jit(solution)/shard_map/dot_general | solution.py:222
  33.9 14.0 %shard_map.155 = (bf16[12,4,16,16,128]{4,3,2,1,0:T(8,128)(2,1)S(1)}, f32[12,4,256,128]{3,2,1,0:T(8,128)}, bf16[12,64,512]{2,1,0:T(8,128)(2,1)S(1)}) custom-call(bf16[12,4,16,16,128]{4,3,2,1,0:T(8,128)(2,1)} %x_ref.3, bf16[12,128,512]{2,1,0:T(8,128)(2,1)S(1)} %bitcast.52, bf16[1152,128]{1,0:T(8,128)(2,1)S(1)} %bitcast.64, f32[1,128]{1,0:T(1,128)S(1)} %bitcast.66), custom_call_target="tpu_custom_call" | custom-call | tf_op jit(solution)/shard_map/pallas_call | solution.py:427
  48.6 0.9 copy-done
  49.5 2.5 %collective-permute-start.9 = (bf16[32,512]{1,0:T(8,128)(2,1)S(1)}, bf16[32,512]{1,0:T(8,128)(2,1)S(1)}, u32[]{:S(2)}, u32[]{:S(2)}) collective-permute-start(bf16[32,512]{1,0:T(8,128)(2,1)S(1)} %get-tuple-element.47), channel_id=1, source_target_pairs={{0,24},{2,26},{4,28},{6,30},{8,0},{10,2},{12,4},{14,6},{16,8},{18,... | collective-permute-start | bytes 98312 | tf_op jit(solution)/shard_map/ppermute | solution.py:21
  52.1 2.3 %collective-permute-start.11 = (bf16[32,512]{1,0:T(8,128)(2,1)S(1)}, bf16[32,512]{1,0:T(8,128)(2,1)S(1)}, u32[]{:S(2)}, u32[]{:S(2)}) collective-permute-start(bf16[32,512]{1,0:T(8,128)(2,1)S(1)} %get-tuple-element.45), channel_id=1, source_target_pairs={{0,28},{2,30},{4,0},{6,2},{8,4},{10,6},{12,8},{14,10},{16,12},{18,... | collective-permute-start | bytes 98312 | tf_op jit(solution)/shard_map/ppermute | solution.py:21
  54.4 2.5 %collective-permute-start.12 = (bf16[224,512]{1,0:T(8,128)(2,1)S(1)}, bf16[224,512]{1,0:T(8,128)(2,1)S(1)}, u32[]{:S(2)}, u32[]{:S(2)}) collective-permute-start(bf16[224,512]{1,0:T(8,128)(2,1)S(1)} %get-tuple-element.49), channel_id=1, source_target_pairs={{0,30},{2,0},{4,2},{6,4},{8,6},{10,8},{12,10},{14,12},{16,14},{18,... | collective-permute-start | bytes 688136 | tf_op jit(solution)/shard_map/ppermute | solution.py:21
  57.0 1.7 collective-permute-start.15
  58.7 1.5 collective-permute-start.16
  60.2 0.9 collective-permute-done.12
  61.1 1.6 collective-permute-start.17
  62.6 3.2 %collective-permute-done.13 = bf16[224,512]{1,0:T(8,128)(2,1)S(1)} collective-permute-done((bf16[224,512]{1,0:T(8,128)(2,1)S(1)}, bf16[224,512]{1,0:T(8,128)(2,1)S(1)}, u32[]{:S(2)}, u32[]{:S(2)}) %collective-permute-start.13) | collective-permute-done | bytes 229408 | tf_op jit(solution)/shard_map/ppermute | solution.py:21
  66.0 2.8 %fusion = bf16[1536,512]{1,0:T(8,128)(2,1)S(1)} fusion(bf16[1424,512]{1,0:T(8,128)(2,1)S(1)} %constant_dynamic-update-slice_fusion.9, s32[1536]{0:T(1024)S(1)} %dynamic-slice_reduce_fusion.1), kind=kOutput, calls=%fused_computation.1 | convolution fusion | flops 2241945600 | bytes 3037184 | tf_op jit(solution)/shard_map/dot_general | solution.py:222
  68.8 34.6 %shard_map.156 = (bf16[12,4,16,16,128]{4,3,2,1,0:T(8,128)(2,1)}, f32[12,4,256,128]{3,2,1,0:T(8,128)}, bf16[12,96,512]{2,1,0:T(8,128)(2,1)S(1)}, f32[128,1152]{1,0:T(8,128)S(1)}, f32[1,128]{1,0:T(1,128)S(1)}) custom-call(bf16[12,4,16,16,128]{4,3,2,1,0:T(8,128)(2,1)} %copy-done, bf16[12,128,512]{2,1,0:T(8,128)(2,1)S(1)} %bitcast.58, ...), custom_call_target="tpu_custom_call" | custom-call | tf_op jit(solution)/shard_map/pallas_call | solution.py:437
  103.3 0.8 copy-done.2
  104.1 1.1 reshape.100
  105.2 1.1 constant_dynamic-update-slice_fusion.28
  106.3 1.1 fusion.5
  107.5 0.9 select_maximum_fusion
  108.4 6.9 %all-to-all-start.2 = ((f32[32,40,128]{2,1,0:T(8,128)}), f32[32,40,128]{2,1,0:T(8,128)S(1)}, u32[]{:S(2)}, u32[]{:S(2)}) async-start(f32[32,40,128]{2,1,0:T(8,128)} %bitcast.23), calls=%async_computation.2 | async-start | bytes 1310720 | tf_op jit(solution)/shard_map/all_to_all | solution.py:482
  115.3 1.6 collective-permute-start.19
  116.9 1.5 collective-permute-start.20
  118.4 4.4 %collective-permute-start.22 = (bf16[224,512]{1,0:T(8,128)(2,1)S(1)}, bf16[224,512]{1,0:T(8,128)(2,1)S(1)}, u32[]{:S(2)}, u32[]{:S(2)}) collective-permute-start(bf16[224,512]{1,0:T(8,128)(2,1)S(1)} %get-tuple-element.40), channel_id=1, source_target_pairs={{0,30},{2,0},{4,2},{6,4},{8,6},{10,8},{12,10},{14,12},{16,14},{18,... | collective-permute-start | bytes 688136 | tf_op jit(solution)/shard_map/ppermute | solution.py:21
  124.0 6.8 %collective-permute-done.19 = bf16[32,512]{1,0:T(8,128)(2,1)S(1)} collective-permute-done((bf16[32,512]{1,0:T(8,128)(2,1)S(1)}, bf16[32,512]{1,0:T(8,128)(2,1)S(1)}, u32[]{:S(2)}, u32[]{:S(2)}) %collective-permute-start.19) | collective-permute-done | bytes 32800 | tf_op jit(solution)/shard_map/ppermute | solution.py:21
  131.4 2.0 collective-permute-done.20
  133.4 3.8 %collective-permute-start.25 = (bf16[32,512]{1,0:T(8,128)(2,1)S(1)}, bf16[32,512]{1,0:T(8,128)(2,1)S(1)}, u32[]{:S(2)}, u32[]{:S(2)}) collective-permute-start(bf16[32,512]{1,0:T(8,128)(2,1)S(1)} %get-tuple-element.34), channel_id=1, source_target_pairs={{0,24},{2,26},{4,28},{6,30},{8,0},{10,2},{12,4},{14,6},{16,8},{18,... | collective-permute-start | bytes 98312 | tf_op jit(solution)/shard_map/ppermute | solution.py:21
  137.8 1.7 collective-permute-start.26
  143.3 3.7 %fusion.2 = f32[768,512]{1,0:T(8,128)S(1)} fusion(bf16[1808,512]{1,0:T(8,128)(2,1)} %constant_dynamic-update-slice_fusion.19, s32[1808]{0:T(1024)S(1)} %dynamic-slice_reduce_fusion), kind=kOutput, calls=%fused_computation.4 | convolution fusion | flops 1423257600 | bytes 3431488 | tf_op jit(solution)/shard_map/dot_general | solution.py:230
  147.0 13.5 %shard_map.157 = (f32[128,1152]{1,0:T(8,128)S(1)}, f32[1,128]{1,0:T(1,128)S(1)}) custom-call(bf16[12,4,16,16,128]{4,3,2,1,0:T(8,128)(2,1)} %x_ref.3, bf16[12,128,512]{2,1,0:T(8,128)(2,1)S(1)} %bitcast.53, f32[12,4,256,128]{3,2,1,0:T(8,128)} %get-tuple-element.18.inner_ref, f32[12,64,512]{2,1,0:T(8,128)S(1)} %bitcast.57, ...), custom_call_target="tpu_custom_call" | custom-call | tf_op jit(solution)/shard_map/pallas_call | solution.py:459
  160.6 0.9 select_maximum_fusion.1
  161.5 3.7 %all-to-all-start = ((f32[32,40,128]{2,1,0:T(8,128)}), f32[32,40,128]{2,1,0:T(8,128)S(1)}, u32[]{:S(2)}, u32[]{:S(2)}) async-start(f32[32,40,128]{2,1,0:T(8,128)} %bitcast.18), calls=%async_computation | async-start | bytes 1310720 | tf_op jit(solution)/shard_map/all_to_all | solution.py:482
  165.3 17.7 %all-to-all-done = f32[32,40,128]{2,1,0:T(8,128)S(1)} async-done(((f32[32,40,128]{2,1,0:T(8,128)}), f32[32,40,128]{2,1,0:T(8,128)S(1)}, u32[]{:S(2)}, u32[]{:S(2)}) %all-to-all-start) | async-done | bytes 655392 | tf_op jit(solution)/shard_map/all_to_all | solution.py:482
  183.8 3.6 %all-to-all-start.3 = ((bf16[32,40,128]{2,1,0:T(8,128)(2,1)}), bf16[32,40,128]{2,1,0:T(8,128)(2,1)S(1)}, u32[]{:S(2)}, u32[]{:S(2)}) async-start(bf16[32,40,128]{2,1,0:T(8,128)(2,1)} %broadcast_in_dim.5), calls=%async_computation.3 | async-start | bytes 655360 | tf_op jit(solution)/shard_map/all_to_all | solution.py:485
  187.5 11.7 %all-to-all-done.3 = bf16[32,40,128]{2,1,0:T(8,128)(2,1)S(1)} async-done(((bf16[32,40,128]{2,1,0:T(8,128)(2,1)}), bf16[32,40,128]{2,1,0:T(8,128)(2,1)S(1)}, u32[]{:S(2)}, u32[]{:S(2)}) %all-to-all-start.3) | async-done | bytes 327712 | tf_op jit(solution)/shard_map/all_to_all | solution.py:485
  199.9 2.7 %all-to-all-start.1 = ((bf16[32,40,128]{2,1,0:T(8,128)(2,1)}), bf16[32,40,128]{2,1,0:T(8,128)(2,1)S(1)}, u32[]{:S(2)}, u32[]{:S(2)}) async-start(bf16[32,40,128]{2,1,0:T(8,128)(2,1)} %broadcast_in_dim.4), calls=%async_computation.1 | async-start | bytes 655360 | tf_op jit(solution)/shard_map/all_to_all | solution.py:485
  203.0 1.1 copy.32
  204.7 9.7 %all-to-all-done.1 = bf16[32,40,128]{2,1,0:T(8,128)(2,1)S(1)} async-done(((bf16[32,40,128]{2,1,0:T(8,128)(2,1)}), bf16[32,40,128]{2,1,0:T(8,128)(2,1)S(1)}, u32[]{:S(2)}, u32[]{:S(2)}) %all-to-all-start.1) | async-done | bytes 327712 | tf_op jit(solution)/shard_map/all_to_all | solution.py:485
  215.2 1.1 copy.31
  (107 shorter events, 20.1 us)
Async XLA Ops:
  6.7 9.0 %copy-start.1 = (bf16[3,3,128,128]{3,2,1,0:T(8,128)(2,1)S(1)}, bf16[3,3,128,128]{3,2,1,0:T(8,128)(2,1)}, u32[]{:S(2)}) copy-start(bf16[3,3,128,128]{3,2,1,0:T(8,128)(2,1)} %param.15) | copy-start | bytes 884740
  6.8 11.2 %collective-permute-start = (bf16[32,512]{1,0:T(8,128)(2,1)S(1)}, bf16[32,512]{1,0:T(8,128)(2,1)S(1)}, u32[]{:S(2)}, u32[]{:S(2)}) collective-permute-start(bf16[32,512]{1,0:T(8,128)(2,1)S(1)} %get-tuple-element.55), channel_id=1, source_target_pairs={{0,24},{2,26},{4,28},{6,30},{8,0},{10,2},{12,4},{14,6},{16,8},{18,... | collective-permute-start | bytes 98312 | tf_op jit(solution)/shard_map/ppermute | solution.py:21
  11.9 7.4 %collective-permute-start.1 = (bf16[32,512]{1,0:T(8,128)(2,1)S(1)}, bf16[32,512]{1,0:T(8,128)(2,1)S(1)}, u32[]{:S(2)}, u32[]{:S(2)}) collective-permute-start(bf16[32,512]{1,0:T(8,128)(2,1)S(1)} %get-tuple-element.54), channel_id=1, source_target_pairs={{0,26},{2,28},{4,30},{6,0},{8,2},{10,4},{12,6},{14,8},{16,10},{18,... | collective-permute-start | bytes 98312 | tf_op jit(solution)/shard_map/ppermute | solution.py:21
  11.9 10.5 %collective-permute-start.2 = (bf16[32,512]{1,0:T(8,128)(2,1)S(1)}, bf16[32,512]{1,0:T(8,128)(2,1)S(1)}, u32[]{:S(2)}, u32[]{:S(2)}) collective-permute-start(bf16[32,512]{1,0:T(8,128)(2,1)S(1)} %get-tuple-element.53), channel_id=1, source_target_pairs={{0,28},{2,30},{4,0},{6,2},{8,4},{10,6},{12,8},{14,10},{16,12},{18,... | collective-permute-start | bytes 98312 | tf_op jit(solution)/shard_map/ppermute | solution.py:21
  13.3 10.9 %collective-permute-start.3 = (bf16[224,512]{1,0:T(8,128)(2,1)S(1)}, bf16[224,512]{1,0:T(8,128)(2,1)S(1)}, u32[]{:S(2)}, u32[]{:S(2)}) collective-permute-start(bf16[224,512]{1,0:T(8,128)(2,1)S(1)} %get-tuple-element.57), channel_id=1, source_target_pairs={{0,30},{2,0},{4,2},{6,4},{8,6},{10,8},{12,10},{14,12},{16,14},{18,... | collective-permute-start | bytes 688136 | tf_op jit(solution)/shard_map/ppermute | solution.py:21
  14.7 11.8 %collective-permute-start.4 = (bf16[224,512]{1,0:T(8,128)(2,1)S(1)}, bf16[224,512]{1,0:T(8,128)(2,1)S(1)}, u32[]{:S(2)}, u32[]{:S(2)}) collective-permute-start(bf16[224,512]{1,0:T(8,128)(2,1)S(1)} %get-tuple-element.56), channel_id=1, source_target_pairs={{0,2},{2,4},{4,6},{6,8},{8,10},{10,12},{12,14},{14,16},{16,18},{18... | collective-permute-start | bytes 688136 | tf_op jit(solution)/shard_map/ppermute | solution.py:21
  17.9 9.3 %collective-permute-start.5 = (bf16[32,512]{1,0:T(8,128)(2,1)S(1)}, bf16[32,512]{1,0:T(8,128)(2,1)S(1)}, u32[]{:S(2)}, u32[]{:S(2)}) collective-permute-start(bf16[32,512]{1,0:T(8,128)(2,1)S(1)} %get-tuple-element.52), channel_id=1, source_target_pairs={{0,4},{2,6},{4,8},{6,10},{8,12},{10,14},{12,16},{14,18},{16,20},{1... | collective-permute-start | bytes 98312 | tf_op jit(solution)/shard_map/ppermute | solution.py:21
  19.2 8.6 %collective-permute-start.6 = (bf16[32,512]{1,0:T(8,128)(2,1)S(1)}, bf16[32,512]{1,0:T(8,128)(2,1)S(1)}, u32[]{:S(2)}, u32[]{:S(2)}) collective-permute-start(bf16[32,512]{1,0:T(8,128)(2,1)S(1)} %get-tuple-element.51), channel_id=1, source_target_pairs={{0,6},{2,8},{4,10},{6,12},{8,14},{10,16},{12,18},{14,20},{16,22},{... | collective-permute-start | bytes 98312 | tf_op jit(solution)/shard_map/ppermute | solution.py:21
  22.3 6.1 %collective-permute-start.7 = (bf16[32,512]{1,0:T(8,128)(2,1)S(1)}, bf16[32,512]{1,0:T(8,128)(2,1)S(1)}, u32[]{:S(2)}, u32[]{:S(2)}) collective-permute-start(bf16[32,512]{1,0:T(8,128)(2,1)S(1)} %get-tuple-element.50), channel_id=1, source_target_pairs={{0,8},{2,10},{4,12},{6,14},{8,16},{10,18},{12,20},{14,22},{16,24},... | collective-permute-start | bytes 98312 | tf_op jit(solution)/shard_map/ppermute | solution.py:21
  24.2 4.9 %collective-permute-start.8 = (bf16[16,512]{1,0:T(8,128)(2,1)S(1)}, bf16[16,512]{1,0:T(8,128)(2,1)S(1)}, u32[]{:S(2)}, u32[]{:S(2)}) collective-permute-start(bf16[16,512]{1,0:T(8,128)(2,1)S(1)} %slice.156), channel_id=1, source_target_pairs={{0,16},{2,18},{4,20},{6,22},{8,24},{10,26},{12,28},{14,30},{16,0},... | collective-permute-start | bytes 49160 | tf_op jit(solution)/shard_map/ppermute | solution.py:21
  29.7 4.2 %copy-start.3 = (bf16[3,3,128,128]{3,2,1,0:T(8,128)(2,1)S(1)}, bf16[3,3,128,128]{3,2,1,0:T(8,128)(2,1)}, u32[]{:S(2)}) copy-start(bf16[3,3,128,128]{3,2,1,0:T(8,128)(2,1)} %param.13) | copy-start | bytes 884740
  29.7 4.2 %copy-start.5 = (f32[128]{0:T(128)S(1)}, f32[128]{0:T(128)}, u32[]{:S(2)}) copy-start(f32[128]{0:T(128)} %param.14) | copy-start | bytes 1540
  47.8 1.6 copy-start
  49.5 7.4 %collective-permute-start.9 = (bf16[32,512]{1,0:T(8,128)(2,1)S(1)}, bf16[32,512]{1,0:T(8,128)(2,1)S(1)}, u32[]{:S(2)}, u32[]{:S(2)}) collective-permute-start(bf16[32,512]{1,0:T(8,128)(2,1)S(1)} %get-tuple-element.47), channel_id=1, source_target_pairs={{0,24},{2,26},{4,28},{6,30},{8,0},{10,2},{12,4},{14,6},{16,8},{18,... | collective-permute-start | bytes 98312 | tf_op jit(solution)/shard_map/ppermute | solution.py:21
  52.1 4.9 %collective-permute-start.10 = (bf16[32,512]{1,0:T(8,128)(2,1)S(1)}, bf16[32,512]{1,0:T(8,128)(2,1)S(1)}, u32[]{:S(2)}, u32[]{:S(2)}) collective-permute-start(bf16[32,512]{1,0:T(8,128)(2,1)S(1)} %get-tuple-element.46), channel_id=1, source_target_pairs={{0,26},{2,28},{4,30},{6,0},{8,2},{10,4},{12,6},{14,8},{16,10},{18,... | collective-permute-start | bytes 98312 | tf_op jit(solution)/shard_map/ppermute | solution.py:21
  52.1 6.5 %collective-permute-start.11 = (bf16[32,512]{1,0:T(8,128)(2,1)S(1)}, bf16[32,512]{1,0:T(8,128)(2,1)S(1)}, u32[]{:S(2)}, u32[]{:S(2)}) collective-permute-start(bf16[32,512]{1,0:T(8,128)(2,1)S(1)} %get-tuple-element.45), channel_id=1, source_target_pairs={{0,28},{2,30},{4,0},{6,2},{8,4},{10,6},{12,8},{14,10},{16,12},{18,... | collective-permute-start | bytes 98312 | tf_op jit(solution)/shard_map/ppermute | solution.py:21
  54.4 6.7 %collective-permute-start.12 = (bf16[224,512]{1,0:T(8,128)(2,1)S(1)}, bf16[224,512]{1,0:T(8,128)(2,1)S(1)}, u32[]{:S(2)}, u32[]{:S(2)}) collective-permute-start(bf16[224,512]{1,0:T(8,128)(2,1)S(1)} %get-tuple-element.49), channel_id=1, source_target_pairs={{0,30},{2,0},{4,2},{6,4},{8,6},{10,8},{12,10},{14,12},{16,14},{18,... | collective-permute-start | bytes 688136 | tf_op jit(solution)/shard_map/ppermute | solution.py:21
  56.9 8.9 %collective-permute-start.13 = (bf16[224,512]{1,0:T(8,128)(2,1)S(1)}, bf16[224,512]{1,0:T(8,128)(2,1)S(1)}, u32[]{:S(2)}, u32[]{:S(2)}) collective-permute-start(bf16[224,512]{1,0:T(8,128)(2,1)S(1)} %get-tuple-element.48), channel_id=1, source_target_pairs={{0,2},{2,4},{4,6},{6,8},{8,10},{10,12},{12,14},{14,16},{16,18},{18... | collective-permute-start | bytes 688136 | tf_op jit(solution)/shard_map/ppermute | solution.py:21
  56.9 8.9 %collective-permute-start.14 = (bf16[32,512]{1,0:T(8,128)(2,1)S(1)}, bf16[32,512]{1,0:T(8,128)(2,1)S(1)}, u32[]{:S(2)}, u32[]{:S(2)}) collective-permute-start(bf16[32,512]{1,0:T(8,128)(2,1)S(1)} %get-tuple-element.44), channel_id=1, source_target_pairs={{0,4},{2,6},{4,8},{6,10},{8,12},{10,14},{12,16},{14,18},{16,20},{1... | collective-permute-start | bytes 98312 | tf_op jit(solution)/shard_map/ppermute | solution.py:21
  57.0 8.9 %collective-permute-start.15 = (bf16[32,512]{1,0:T(8,128)(2,1)S(1)}, bf16[32,512]{1,0:T(8,128)(2,1)S(1)}, u32[]{:S(2)}, u32[]{:S(2)}) collective-permute-start(bf16[32,512]{1,0:T(8,128)(2,1)S(1)} %get-tuple-element.43), channel_id=1, source_target_pairs={{0,6},{2,8},{4,10},{6,12},{8,14},{10,16},{12,18},{14,20},{16,22},{... | collective-permute-start | bytes 98312 | tf_op jit(solution)/shard_map/ppermute | solution.py:21
  58.7 7.2 %collective-permute-start.16 = (bf16[32,512]{1,0:T(8,128)(2,1)S(1)}, bf16[32,512]{1,0:T(8,128)(2,1)S(1)}, u32[]{:S(2)}, u32[]{:S(2)}) collective-permute-start(bf16[32,512]{1,0:T(8,128)(2,1)S(1)} %get-tuple-element.42), channel_id=1, source_target_pairs={{0,8},{2,10},{4,12},{6,14},{8,16},{10,18},{12,20},{14,22},{16,24},... | collective-permute-start | bytes 98312 | tf_op jit(solution)/shard_map/ppermute | solution.py:21
  61.1 4.9 %collective-permute-start.17 = (bf16[16,512]{1,0:T(8,128)(2,1)S(1)}, bf16[16,512]{1,0:T(8,128)(2,1)S(1)}, u32[]{:S(2)}, u32[]{:S(2)}) collective-permute-start(bf16[16,512]{1,0:T(8,128)(2,1)S(1)} %slice.165), channel_id=1, source_target_pairs={{0,16},{2,18},{4,20},{6,22},{8,24},{10,26},{12,28},{14,30},{16,0},... | collective-permute-start | bytes 49160 | tf_op jit(solution)/shard_map/ppermute | solution.py:21
  66.0 2.8 %copy-start.4 = (f32[128]{0:T(128)S(1)}, f32[128]{0:T(128)}, u32[]{:S(2)}) copy-start(f32[128]{0:T(128)} %param.16) | copy-start | bytes 1540
  103.3 0.8 copy-start.2
  107.4 15.4 %collective-permute-start.18 = (bf16[32,512]{1,0:T(8,128)(2,1)S(1)}, bf16[32,512]{1,0:T(8,128)(2,1)S(1)}, u32[]{:S(2)}, u32[]{:S(2)}) collective-permute-start(bf16[32,512]{1,0:T(8,128)(2,1)S(1)} %get-tuple-element.39), channel_id=1, source_target_pairs={{0,8},{2,10},{4,12},{6,14},{8,16},{10,18},{12,20},{14,22},{16,24},... | collective-permute-start | bytes 98312 | tf_op jit(solution)/shard_map/ppermute | solution.py:21
  108.4 53.1 %all-to-all-start.2 = ((f32[32,40,128]{2,1,0:T(8,128)}), f32[32,40,128]{2,1,0:T(8,128)S(1)}, u32[]{:S(2)}, u32[]{:S(2)}) async-start(f32[32,40,128]{2,1,0:T(8,128)} %bitcast.23), calls=%async_computation.2 | async-start | bytes 1310720 | tf_op jit(solution)/shard_map/all_to_all | solution.py:482
  115.3 15.5 %collective-permute-start.19 = (bf16[32,512]{1,0:T(8,128)(2,1)S(1)}, bf16[32,512]{1,0:T(8,128)(2,1)S(1)}, u32[]{:S(2)}, u32[]{:S(2)}) collective-permute-start(bf16[32,512]{1,0:T(8,128)(2,1)S(1)} %get-tuple-element.38), channel_id=1, source_target_pairs={{0,6},{2,8},{4,10},{6,12},{8,14},{10,16},{12,18},{14,20},{16,22},{... | collective-permute-start | bytes 98312 | tf_op jit(solution)/shard_map/ppermute | solution.py:21
  116.9 16.5 %collective-permute-start.20 = (bf16[32,512]{1,0:T(8,128)(2,1)S(1)}, bf16[32,512]{1,0:T(8,128)(2,1)S(1)}, u32[]{:S(2)}, u32[]{:S(2)}) collective-permute-start(bf16[32,512]{1,0:T(8,128)(2,1)S(1)} %get-tuple-element.37), channel_id=1, source_target_pairs={{0,4},{2,6},{4,8},{6,10},{8,12},{10,14},{12,16},{14,18},{16,20},{1... | collective-permute-start | bytes 98312 | tf_op jit(solution)/shard_map/ppermute | solution.py:21
  118.4 19.4 %collective-permute-start.21 = (bf16[224,512]{1,0:T(8,128)(2,1)S(1)}, bf16[224,512]{1,0:T(8,128)(2,1)S(1)}, u32[]{:S(2)}, u32[]{:S(2)}) collective-permute-start(bf16[224,512]{1,0:T(8,128)(2,1)S(1)} %get-tuple-element.41), channel_id=1, source_target_pairs={{0,2},{2,4},{4,6},{6,8},{8,10},{10,12},{12,14},{14,16},{16,18},{18... | collective-permute-start | bytes 688136 | tf_op jit(solution)/shard_map/ppermute | solution.py:21
  118.4 21.8 %collective-permute-start.22 = (bf16[224,512]{1,0:T(8,128)(2,1)S(1)}, bf16[224,512]{1,0:T(8,128)(2,1)S(1)}, u32[]{:S(2)}, u32[]{:S(2)}) collective-permute-start(bf16[224,512]{1,0:T(8,128)(2,1)S(1)} %get-tuple-element.40), channel_id=1, source_target_pairs={{0,30},{2,0},{4,2},{6,4},{8,6},{10,8},{12,10},{14,12},{16,14},{18,... | collective-permute-start | bytes 688136 | tf_op jit(solution)/shard_map/ppermute | solution.py:21
  122.8 18.1 %collective-permute-start.23 = (bf16[32,512]{1,0:T(8,128)(2,1)S(1)}, bf16[32,512]{1,0:T(8,128)(2,1)S(1)}, u32[]{:S(2)}, u32[]{:S(2)}) collective-permute-start(bf16[32,512]{1,0:T(8,128)(2,1)S(1)} %get-tuple-element.36), channel_id=1, source_target_pairs={{0,28},{2,30},{4,0},{6,2},{8,4},{10,6},{12,8},{14,10},{16,12},{18,... | collective-permute-start | bytes 98312 | tf_op jit(solution)/shard_map/ppermute | solution.py:21
  130.8 10.7 %collective-permute-start.24 = (bf16[32,512]{1,0:T(8,128)(2,1)S(1)}, bf16[32,512]{1,0:T(8,128)(2,1)S(1)}, u32[]{:S(2)}, u32[]{:S(2)}) collective-permute-start(bf16[32,512]{1,0:T(8,128)(2,1)S(1)} %get-tuple-element.35), channel_id=1, source_target_pairs={{0,26},{2,28},{4,30},{6,0},{8,2},{10,4},{12,6},{14,8},{16,10},{18,... | collective-permute-start | bytes 98312 | tf_op jit(solution)/shard_map/ppermute | solution.py:21
  133.4 8.8 %collective-permute-start.25 = (bf16[32,512]{1,0:T(8,128)(2,1)S(1)}, bf16[32,512]{1,0:T(8,128)(2,1)S(1)}, u32[]{:S(2)}, u32[]{:S(2)}) collective-permute-start(bf16[32,512]{1,0:T(8,128)(2,1)S(1)} %get-tuple-element.34), channel_id=1, source_target_pairs={{0,24},{2,26},{4,28},{6,30},{8,0},{10,2},{12,4},{14,6},{16,8},{18,... | collective-permute-start | bytes 98312 | tf_op jit(solution)/shard_map/ppermute | solution.py:21
  137.8 5.0 %collective-permute-start.26 = (bf16[16,512]{1,0:T(8,128)(2,1)S(1)}, bf16[16,512]{1,0:T(8,128)(2,1)S(1)}, u32[]{:S(2)}, u32[]{:S(2)}) collective-permute-start(bf16[16,512]{1,0:T(8,128)(2,1)S(1)} %slice.176), channel_id=1, source_target_pairs={{0,16},{2,18},{4,20},{6,22},{8,24},{10,26},{12,28},{14,30},{16,0},... | collective-permute-start | bytes 49160 | tf_op jit(solution)/shard_map/ppermute | solution.py:21
  161.5 21.6 %all-to-all-start = ((f32[32,40,128]{2,1,0:T(8,128)}), f32[32,40,128]{2,1,0:T(8,128)S(1)}, u32[]{:S(2)}, u32[]{:S(2)}) async-start(f32[32,40,128]{2,1,0:T(8,128)} %bitcast.18), calls=%async_computation | async-start | bytes 1310720 | tf_op jit(solution)/shard_map/all_to_all | solution.py:482
  183.8 15.3 %all-to-all-start.3 = ((bf16[32,40,128]{2,1,0:T(8,128)(2,1)}), bf16[32,40,128]{2,1,0:T(8,128)(2,1)S(1)}, u32[]{:S(2)}, u32[]{:S(2)}) async-start(bf16[32,40,128]{2,1,0:T(8,128)(2,1)} %broadcast_in_dim.5), calls=%async_computation.3 | async-start | bytes 655360 | tf_op jit(solution)/shard_map/all_to_all | solution.py:485
  199.9 14.4 %all-to-all-start.1 = ((bf16[32,40,128]{2,1,0:T(8,128)(2,1)}), bf16[32,40,128]{2,1,0:T(8,128)(2,1)S(1)}, u32[]{:S(2)}, u32[]{:S(2)}) async-start(bf16[32,40,128]{2,1,0:T(8,128)(2,1)} %broadcast_in_dim.4), calls=%async_computation.1 | async-start | bytes 655360 | tf_op jit(solution)/shard_map/all_to_all | solution.py:485
